TPU v7x, 256 devices: a whole 4x4x8 slice. The times are simulated.
256 devices in a mesh: seq: 64 (over z, x, core), mp: 4 (over y).
Axes of the slice: x: 4, y: 4, z: 8, core: 2. Of those that a mesh axis runs over, the one named last changes fastest.
Arguments:
- tiles: bfloat16 [32768, 768], P('seq'), may hold values from -6 to 6
- w_qkv: bfloat16 [768, 2304], P(None, 'mp'), may hold values from -0.3125 to 0.3125
- w_out: bfloat16 [768, 768], P('mp'), may hold values from -0.4375 to 0.4375
- slide_lengths: int32 [4], replicated, may hold values from 1 to 16384, 32768 in all
- drop_salt: int32 [1], replicated, may hold values from 0 to 1048575
- cotangent: bfloat16 [32768, 768], P('seq'), may hold values from -6 to 6
Outputs:
- layer_out: bfloat16 [32768, 768], P('seq')
- tile_gradient: bfloat16 [32768, 768], P('seq')
- grad_w_qkv: float32 [768, 2304], P(None, 'mp')
- grad_w_out: float32 [768, 768], P('mp')
Inputs may be any that keep to these rules, and one draw needn't show every extreme that they name: `slide_lengths`: the four lengths sum to 32768; the longest slide holds exactly 16384 tiles.
All inputs are finite; a program needn't handle non-finite values.
Results may differ from a plain program's by a relative error of at most 0.017.
Values may be sent and summed in bfloat16 or wider, within the bound.
No kernel may reach another device: no remote copies, remote signals or barrier semaphores. Data moves between devices by JAX's collectives and lax.ppermute only.
A program may use at most 128 MiB of HBM per device.

v0:
```python
import jax
import jax.numpy as jnp
from jax import lax
from jax.sharding import PartitionSpec as P

SEG_LOCAL = 512
G_NEAR = 4


drop_scale = 1024.0 / 922.0


def swapped(block, axis, apart):
    count = lax.axis_size(axis)
    route = []
    for low in range(count):
        high = low | 1 << apart
        if high != low and high < count:
            route += [(low, high), (high, low)]
    return lax.ppermute(block, axis, route)


def keep_mask(salt, positions, features, width):
    index = positions * width + features
    mixed = index * 747796405 + salt
    mixed = mixed ^ mixed >> 13
    mixed = mixed * 1274126177
    mixed = mixed ^ mixed >> 16
    return mixed & 1023 >= 102


def slide_of(positions, slide_lengths):
    ends = jnp.cumsum(slide_lengths)
    return jnp.sum((positions[..., None] >= ends[:3]).astype(jnp.int32), -1)


def weights_of(queries, keys_in, query_slide, key_slide):
    factor = queries.shape[-1] ** (-0.5)
    scores = (
        jnp.einsum("bqhd,bkhd->bhqk", queries, keys_in, preferred_element_type=jnp.float32) * factor
    )
    allowed = query_slide[:, :, :, None] == key_slide[:, :, None, :]
    return jnp.exp(jnp.where(allowed, scores, -1e30))


def stats_pass(queries, keys_in, values_in, query_slide, key_slide):
    weights = weights_of(queries, keys_in, query_slide, key_slide)
    totals = jnp.swapaxes(jnp.sum(weights, -1), 1, 2)
    numer = jnp.einsum(
        "bhqk,bkhd->bqhd", weights, values_in.astype(jnp.float32), precision=lax.Precision.HIGHEST
    )
    return (totals, numer)


def grad_pass(queries, keys_in, values_in, grad_out, query_slide, key_slide, totals, delta):
    factor = queries.shape[-1] ** (-0.5)
    weights = weights_of(queries, keys_in, query_slide, key_slide)
    shares = weights / jnp.swapaxes(totals, 1, 2)[..., None]
    shares_low = shares.astype(jnp.bfloat16)
    outputs = jnp.einsum(
        "bhqk,bkhd->bqhd", shares_low, values_in, preferred_element_type=jnp.float32
    )
    grad_values = jnp.einsum(
        "bhqk,bqhd->bkhd", shares_low, grad_out, preferred_element_type=jnp.float32
    )
    grad_shares = jnp.einsum(
        "bqhd,bkhd->bhqk", grad_out, values_in, preferred_element_type=jnp.float32
    )
    centred = grad_shares - jnp.swapaxes(delta, 1, 2)[..., None]
    grad_scores = (shares * centred).astype(jnp.bfloat16)
    grad_queries = (
        jnp.einsum("bhqk,bkhd->bqhd", grad_scores, keys_in, preferred_element_type=jnp.float32)
        * factor
    )
    grad_keys = (
        jnp.einsum("bhqk,bqhd->bkhd", grad_scores, queries, preferred_element_type=jnp.float32)
        * factor
    )
    return (outputs, grad_queries, grad_keys, grad_values)


def pick_heads(array, rate, offsets):
    count = array.shape[0] // rate
    shaped = array.reshape((count, rate) + array.shape[1:])
    return jnp.stack(
        [
            lax.dynamic_index_in_dim(
                shaped[:, :, head_index], offsets[head_index], 1, keepdims=False
            )
            for head_index in range(4)
        ],
        1,
    )


def spread_heads(selected, rate, offset_array):
    chosen = jnp.arange(rate, dtype=jnp.int32)[:, None] == offset_array[None, :]
    shape = (1, rate, 4) + (1,) * (selected.ndim - 2)
    filled = jnp.where(chosen.reshape(shape), selected[:, None], jnp.zeros((), selected.dtype))
    return filled.reshape((selected.shape[0] * rate,) + selected.shape[1:])


def collect_swaps(local_rows, group, place):
    gathered = local_rows
    for bit_index in range(group.bit_length() - 1):
        partner = swapped(gathered, "seq", bit_index)
        upper_bit = place >> bit_index & 1
        gathered = jnp.where(
            upper_bit == 0,
            jnp.concatenate([gathered, partner], 0),
            jnp.concatenate([partner, gathered], 0),
        )
    return gathered


def return_swaps(group_rows, group, place):
    kept_rows = group_rows
    for bit_index in reversed(range(group.bit_length() - 1)):
        middle = kept_rows.shape[0] // 2
        lower_half = kept_rows[:middle]
        upper_half = kept_rows[middle:]
        mine_upper = place >> bit_index & 1 == 1
        outgoing = jnp.where(mine_upper, lower_half, upper_half)
        staying = jnp.where(mine_upper, upper_half, lower_half)
        kept_rows = staying + swapped(outgoing.astype(jnp.bfloat16), "seq", bit_index).astype(
            outgoing.dtype
        )
    return kept_rows


def collect_whole(local_rows, groups, place):
    return collect_swaps(local_rows, groups, place)


def return_whole(group_rows, groups, place):
    return return_swaps(group_rows, groups, place)


def shards(tiles, w_qkv, w_out, slide_lengths, drop_salt, cotangent):
    tok_rows, width = tiles.shape
    head_size = width // 16
    member = lax.axis_index("mp")
    place = lax.axis_index("seq")
    groups = lax.axis_size("seq")
    wide = tiles.astype(jnp.float32)
    centered_input = wide - jnp.mean(wide, -1, keepdims=True)
    inverse_deviation = lax.rsqrt(
        jnp.mean(centered_input * centered_input, -1, keepdims=True) + 1e-05
    )
    standardized_input = centered_input * inverse_deviation
    normalized_rows = standardized_input.astype(jnp.bfloat16)
    qkv = jnp.dot(normalized_rows, w_qkv, preferred_element_type=jnp.float32).astype(jnp.bfloat16)
    qkv = qkv.reshape(tok_rows, 3, 4, head_size)
    by_head = jnp.swapaxes(qkv, 1, 2)
    positions = place * tok_rows + jnp.arange(tok_rows, dtype=jnp.int32)
    slide = slide_of(positions, slide_lengths)
    keeper = keep_mask(
        drop_salt[0], positions[:, None], jnp.arange(width, dtype=jnp.int32)[None, :], width
    )
    drop_factor = jnp.where(keeper, drop_scale, 0.0).astype(jnp.float32)
    grad_branch = (cotangent.astype(jnp.float32) * drop_factor).astype(jnp.bfloat16)
    grad_heads = jnp.einsum("td,hd->th", grad_branch, w_out, preferred_element_type=jnp.float32)
    grad_heads = grad_heads.astype(jnp.bfloat16).reshape(tok_rows, 4, head_size)
    blocks = tok_rows // SEG_LOCAL

    def blocked(array):
        return array.reshape((blocks, SEG_LOCAL) + array.shape[1:])

    local_q = blocked(qkv[:, 0])
    local_k = blocked(qkv[:, 1])
    local_v = blocked(qkv[:, 2])
    local_slide = jnp.broadcast_to(blocked(slide)[:, None, :], (blocks, 4, SEG_LOCAL))
    local_totals, local_numer = stats_pass(local_q, local_k, local_v, local_slide, local_slide)
    total_all = local_totals.reshape(tok_rows, 4)
    numer_all = local_numer.reshape(tok_rows, 4, head_size)
    stored = []
    for rate in (G_NEAR, min(16, groups), groups):
        offsets = [(4 * member + head_index) % rate for head_index in range(4)]
        offset_array = jnp.stack(offsets)
        count = tok_rows // rate
        picked = pick_heads(by_head, rate, offsets)
        queries = picked[:, :, 0]
        joined_local = jnp.swapaxes(picked[:, :, 1:], 1, 2).reshape(count, 8 * head_size)
        if rate < groups:
            joined = collect_swaps(joined_local, rate, place)
        else:
            joined = collect_whole(joined_local, groups, place)
        slots = jnp.arange(tok_rows, dtype=jnp.int32)
        first_device = place // rate * rate
        key_base = (first_device + slots // count) * tok_rows + slots % count * rate
        key_slide = slide_of(key_base[None, :] + offset_array[:, None], slide_lengths)
        query_base = place * tok_rows + jnp.arange(count, dtype=jnp.int32) * rate
        query_slide = slide_of(query_base[None, :] + offset_array[:, None], slide_lengths)
        shaped_keys = joined.reshape(tok_rows, 2, 4, head_size)
        keys_in = shaped_keys[:, 0]
        values_in = shaped_keys[:, 1]
        totals, numer = stats_pass(
            queries[None], keys_in[None], values_in[None], query_slide[None], key_slide[None]
        )
        total_all = total_all + spread_heads(totals[0], rate, offset_array)
        numer_all = numer_all + spread_heads(numer[0], rate, offset_array)
        stored.append(
            (rate, offsets, offset_array, queries, keys_in, values_in, query_slide, key_slide)
        )
    mixed = numer_all / total_all[..., None]
    delta = jnp.sum(grad_heads.astype(jnp.float32) * mixed, -1)
    outputs, grad_q, grad_k, grad_v = grad_pass(
        local_q,
        local_k,
        local_v,
        blocked(grad_heads),
        local_slide,
        local_slide,
        blocked(total_all),
        blocked(delta),
    )
    out_total = outputs.reshape(tok_rows, 4, head_size)
    query_total = grad_q.reshape(tok_rows, 4, head_size)
    key_total = grad_k.reshape(tok_rows, 4, head_size)
    value_total = grad_v.reshape(tok_rows, 4, head_size)
    for rate, offsets, offset_array, queries, keys_in, values_in, query_slide, key_slide in stored:
        count = tok_rows // rate
        grad_out = pick_heads(grad_heads, rate, offsets)
        outputs, grad_q, grad_k, grad_v = grad_pass(
            queries[None],
            keys_in[None],
            values_in[None],
            grad_out[None],
            query_slide[None],
            key_slide[None],
            pick_heads(total_all, rate, offsets)[None],
            pick_heads(delta, rate, offsets)[None],
        )
        partial_rows = jnp.stack([grad_k[0], grad_v[0]], 1).reshape(tok_rows, 8 * head_size)
        if rate < groups:
            own_rows = return_swaps(partial_rows, rate, place)
        else:
            own_rows = return_whole(partial_rows, groups, place)
        own_rows = own_rows.reshape(count, 2, 4, head_size)
        out_total = out_total + spread_heads(outputs[0], rate, offset_array)
        query_total = query_total + spread_heads(grad_q[0], rate, offset_array)
        key_total = key_total + spread_heads(own_rows[:, 0], rate, offset_array)
        value_total = value_total + spread_heads(own_rows[:, 1], rate, offset_array)
    heads_flat = out_total.astype(jnp.bfloat16).reshape(tok_rows, 4 * head_size)
    grad_qkv = jnp.stack([query_total, key_total, value_total], 1).astype(jnp.bfloat16)
    grad_qkv = grad_qkv.reshape(tok_rows, 12 * head_size)
    proj = lax.psum(
        jnp.dot(heads_flat, w_out, preferred_element_type=jnp.float32).astype(jnp.bfloat16), "mp"
    ).astype(jnp.float32)
    layer_out = (proj * drop_factor).astype(jnp.bfloat16)
    inv_rows = (tok_rows * groups) ** (-0.5)
    term_qkv = jnp.einsum(
        "td,tc->dc", normalized_rows, grad_qkv, preferred_element_type=jnp.float32
    )
    term_out = jnp.einsum("th,td->hd", heads_flat, grad_branch, preferred_element_type=jnp.float32)
    summed_qkv, summed_out = lax.psum((term_qkv, term_out), "seq")
    back_term = jnp.einsum("tc,dc->td", grad_qkv, w_qkv, preferred_element_type=jnp.float32)
    normalized_gradient = lax.psum(back_term.astype(jnp.bfloat16), "mp").astype(jnp.float32)
    gradient_mean = jnp.mean(normalized_gradient, -1, keepdims=True)
    mixed_product_mean = jnp.mean(normalized_gradient * standardized_input, -1, keepdims=True)
    tile_gradient = (
        inverse_deviation
        * (normalized_gradient - gradient_mean - standardized_input * mixed_product_mean)
    ).astype(jnp.bfloat16)
    return (layer_out, tile_gradient, summed_qkv * inv_rows, summed_out * inv_rows)


def solution(mesh):
    placed = (P("seq", None), P(None, "mp"), P("mp", None), P(), P(), P("seq", None))
    return jax.shard_map(
        shards,
        mesh=mesh,
        in_specs=placed,
        out_specs=(P("seq", None), P("seq", None), P(None, "mp"), P("mp", None)),
        check_vma=False,
    )
```

profile of v0, /device:TPU:1, one launch (start us, length us, event | category | flops | bytes accessed | tf_op | source)
XLA Modules:
  0.0 504.7 jit_solution(17539424058461744632)
XLA Ops:
  7.3 1.4 convert_reduce_fusion.1
  8.7 1.5 fusion.13
  16.2 3.2 collective-permute-start.6
  19.5 1.8 copy.167
  21.2 1.6 fusion.140
  22.8 2.2 constant_dynamic-slice_fusion.30
  26.2 2.2 constant_dynamic-slice_fusion.28
  28.4 1.6 copy.171
  30.8 1.4 pad_maximum_fusion.7
  38.2 2.2 convolution_convert_fusion.3
  41.7 1.4 fusion.180
  43.1 1.5 fusion.181
  56.7 3.2 fusion.2
  78.6 2.0 collective-permute-start.8
  83.2 1.7 collective-permute-start.9
  85.7 2.3 collective-permute-start.4
  88.2 2.1 collective-permute-start.10
  90.6 1.8 maximum_select_fusion.4
  94.8 1.5 collective-permute-start.5
  97.7 4.6 collective-permute-start.11
  103.7 2.0 fusion.156
  105.6 1.3 convolution_bitcast_fusion.4
  107.0 1.7 copy.202
  108.7 1.5 broadcast_in_dim.474
  110.2 1.7 broadcast_in_dim.532
  124.4 5.1 %fusion.61 = f32[512,4]{0,1:T(4,128)S(1)} fusion(f32[4,512,512]{1,2,0:T(8,128)} %get-tuple-element.76, pred[512,512]{0,1:T(8,128)(4,1)} %copy-done.70, f32[512,4,48]{0,2,1:T(8,128)} %broadcast_in_dim.531, f32[512,4,48]{0,2,1:T(8,128)} %copy.204, f32[512,4,48]{0,2,1:T(8,128)} %copy.203, bf16[512,4,48]{0,2,1:T(8,128)(2,1)S(1)} %bitcast.554, ...), kind=kOutput, calls=%fused_computation.100 | convolution fusion | flops 607057920 | bytes 6051840 | tf_op jit(solution)/shard_map/bhqk,bkhd->bqhd/dot_general | solution.py:49
  139.7 1.8 convolution_bitcast_fusion.6
  163.6 3.4 fusion.57
  168.8 1.7 copy.193
  179.4 5.0 multiply_convert_fusion
  187.1 1.9 add_convert_fusion
  189.7 1.9 fusion.63
  194.9 2.0 collective-permute-start.15
  199.7 4.4 collective-permute-start.13
  214.8 2.7 collective-permute-start.21
  218.6 2.4 collective-permute-start.17
  222.3 2.4 collective-permute-done.22
  225.6 4.9 collective-permute-start.23
  238.6 4.1 fusion.44
  243.8 2.0 fusion.135
  248.0 1.7 convolution_convert_fusion
  249.8 183.8 %all-reduce.5.cloned.1.call-done = (f32[768,576]{0,1:T(8,128)}, f32[192,768]{1,0:T(8,128)}) async-done(((f32[768,576]{0,1:T(8,128)}, f32[192,768]{1,0:T(8,128)}), (f32[768,576]{0,1:T(8,128)}, f32[192,768]{1,0:T(8,128)})) %all-reduce.5.cloned.1.call-update) | async-done | bytes 2359312 | tf_op jit(solution)/shard_map/psum | solution.py:256
  433.5 1.9 broadcast_multiply_fusion.1
  435.5 2.8 broadcast_multiply_fusion
  438.3 54.3 %all-reduce.7.cloned.1.call-done = (bf16[512,768]{1,0:T(8,128)(2,1)}, bf16[512,768]{1,0:T(8,128)(2,1)}) async-done(((bf16[512,768]{1,0:T(8,128)(2,1)}, bf16[512,768]{1,0:T(8,128)(2,1)}), (bf16[512,768]{1,0:T(8,128)(2,1)}, bf16[512,768]{1,0:T(8,128)(2,1)})) %all-reduce.7.cloned.1.call-update) | async-done | bytes 1572880 | tf_op jit(solution)/shard_map/psum | solution.py:247
  492.6 2.0 convert_reduce_fusion
  494.6 1.6 fusion.14
  496.3 1.4 fusion.12
  (593 shorter events, 142.9 us)
Async XLA Ops:
  7.2 426.4 %all-reduce.5.cloned.1.call-start = ((), (), s32[]{:S(2)}) async-start(), calls=%async_computation | async-start | bytes 4718592 | tf_op jit(solution)/shard_map/psum | solution.py:256
  16.2 45.1 %collective-permute-start.6 = (bf16[8,384]{1,0:T(8,128)(2,1)}, bf16[8,384]{1,0:T(8,128)(2,1)}, u32[]{:S(2)}, u32[]{:S(2)}) collective-permute-start(bf16[8,384]{1,0:T(8,128)(2,1)} %reshape.1243), channel_id=1, source_target_pairs={{0,4},{4,0},{8,12},{12,8},{16,20},{20,16},{24,28},{28,24},{32,36},... | collective-permute-start | bytes 18440 | tf_op jit(solution)/shard_map/ppermute | solution.py:20
  26.2 15.5 %copy-start.41 = (bf16[128,1,1,3,48]{0,4,3,2,1:T(8,128)(2,1)}, bf16[128,1,1,3,48]{0,4,3,2,1:T(8,128)(2,1)S(1)}, u32[]{:S(2)}) copy-start(bf16[128,1,1,3,48]{0,4,3,2,1:T(8,128)(2,1)S(1)} %copy.168) | copy-start | bytes 110596
  32.2 58.4 %collective-permute-start = (bf16[128,384]{0,1:T(8,128)(2,1)}, bf16[128,384]{0,1:T(8,128)(2,1)}, u32[]{:S(2)}, u32[]{:S(2)}) collective-permute-start(bf16[128,384]{0,1:T(8,128)(2,1)} %bitcast.24), channel_id=1, source_target_pairs={{0,4},{4,0},{8,12},{12,8},{16,20},{20,16},{24,28},{28,24},{32,36},... | collective-permute-start | bytes 294920 | tf_op jit(solution)/shard_map/ppermute | solution.py:20
  36.9 43.9 %collective-permute-start.2 = (bf16[32,384]{0,1:T(8,128)(2,1)}, bf16[32,384]{0,1:T(8,128)(2,1)}, u32[]{:S(2)}, u32[]{:S(2)}) collective-permute-start(bf16[32,384]{0,1:T(8,128)(2,1)} %bitcast.44), channel_id=1, source_target_pairs={{0,4},{4,0},{8,12},{12,8},{16,20},{20,16},{24,28},{28,24},{32,36},... | collective-permute-start | bytes 73736 | tf_op jit(solution)/shard_map/ppermute | solution.py:20
  48.6 8.0 %copy-start.70 = (pred[512,512]{0,1:T(8,128)(4,1)}, pred[512,512]{0,1:T(8,128)(4,1)S(1)}, u32[]{:S(2)}) copy-start(pred[512,512]{0,1:T(8,128)(4,1)S(1)} %broadcast_compare_fusion) | copy-start | bytes 786436
  56.7 11.0 %copy-start.132 = (pred[4,4]{0,1:T(4,128)(4,1)S(1)}, pred[4,4]{0,1:T(4,128)(4,1)}, u32[]{:S(2)}) copy-start(pred[4,4]{0,1:T(4,128)(4,1)} %iota_compare_fusion.2) | copy-start | bytes 52
  59.9 12.2 %copy-start.55 = (bf16[8,1,1,48]{1,0,3,2:T(8,128)(2,1)S(1)}, bf16[8,1,1,48]{1,0,3,2:T(8,128)(2,1)}, u32[]{:S(2)}) copy-start(bf16[8,1,1,48]{1,0,3,2:T(8,128)(2,1)} %constant_dynamic-slice_fusion.5) | copy-start | bytes 2308
  59.9 12.9 %copy-start.56 = (bf16[8,1,1,48]{1,0,3,2:T(8,128)(2,1)S(1)}, bf16[8,1,1,48]{1,0,3,2:T(8,128)(2,1)}, u32[]{:S(2)}) copy-start(bf16[8,1,1,48]{1,0,3,2:T(8,128)(2,1)} %constant_dynamic-slice_fusion.6) | copy-start | bytes 2308
  59.9 13.6 %copy-start.73 = (bf16[128,1,1,48]{3,2,1,0:T(2,128)(2,1)S(1)}, bf16[128,1,1,48]{3,2,1,0:T(2,128)(2,1)}, u32[]{:S(2)}) copy-start(bf16[128,1,1,48]{3,2,1,0:T(2,128)(2,1)} %constant_dynamic-slice_fusion.15) | copy-start | bytes 36868
  59.9 14.3 %copy-start.74 = (bf16[128,1,1,48]{3,2,1,0:T(2,128)(2,1)S(1)}, bf16[128,1,1,48]{3,2,1,0:T(2,128)(2,1)}, u32[]{:S(2)}) copy-start(bf16[128,1,1,48]{3,2,1,0:T(2,128)(2,1)} %constant_dynamic-slice_fusion.12) | copy-start | bytes 36868
  59.9 14.9 %copy-start.75 = (bf16[128,1,1,48]{3,2,1,0:T(2,128)(2,1)S(1)}, bf16[128,1,1,48]{3,2,1,0:T(2,128)(2,1)}, u32[]{:S(2)}) copy-start(bf16[128,1,1,48]{3,2,1,0:T(2,128)(2,1)} %constant_dynamic-slice_fusion.13) | copy-start | bytes 36868
  59.9 15.6 %copy-start.76 = (bf16[128,1,1,48]{3,2,1,0:T(2,128)(2,1)S(1)}, bf16[128,1,1,48]{3,2,1,0:T(2,128)(2,1)}, u32[]{:S(2)}) copy-start(bf16[128,1,1,48]{3,2,1,0:T(2,128)(2,1)} %constant_dynamic-slice_fusion.14) | copy-start | bytes 36868
  59.9 16.3 %copy-start.82 = (bf16[32,1,1,48]{3,2,1,0:T(2,128)(2,1)S(1)}, bf16[32,1,1,48]{3,2,1,0:T(2,128)(2,1)}, u32[]{:S(2)}) copy-start(bf16[32,1,1,48]{3,2,1,0:T(2,128)(2,1)} %constant_dynamic-slice_fusion.11) | copy-start | bytes 9220
  59.9 16.9 %copy-start.83 = (bf16[32,1,1,48]{3,2,1,0:T(2,128)(2,1)S(1)}, bf16[32,1,1,48]{3,2,1,0:T(2,128)(2,1)}, u32[]{:S(2)}) copy-start(bf16[32,1,1,48]{3,2,1,0:T(2,128)(2,1)} %constant_dynamic-slice_fusion.8) | copy-start | bytes 9220
  60.0 17.5 %copy-start.84 = (bf16[32,1,1,48]{3,2,1,0:T(2,128)(2,1)S(1)}, bf16[32,1,1,48]{3,2,1,0:T(2,128)(2,1)}, u32[]{:S(2)}) copy-start(bf16[32,1,1,48]{3,2,1,0:T(2,128)(2,1)} %constant_dynamic-slice_fusion.9) | copy-start | bytes 9220
  60.0 22.1 %copy-start.61 = (bf16[32,2,4,48]{0,3,2,1:T(8,128)(2,1)S(1)}, bf16[32,2,4,48]{0,3,2,1:T(8,128)(2,1)}, u32[]{:S(2)}) copy-start(bf16[32,2,4,48]{0,3,2,1:T(8,128)(2,1)} %fusion.181) | copy-start | bytes 73732
  62.1 16.5 %collective-permute-start.7 = (bf16[16,384]{1,0:T(8,128)(2,1)S(1)}, bf16[16,384]{1,0:T(8,128)(2,1)S(1)}, u32[]{:S(2)}, u32[]{:S(2)}) collective-permute-start(bf16[16,384]{1,0:T(8,128)(2,1)S(1)} %maximum_select_fusion.18), channel_id=1, source_target_pairs={{0,8},{8,0},{4,12},{12,4},{16,24},{24,16},{20,28},{28,20},{32,40},... | collective-permute-start | bytes 36872 | tf_op jit(solution)/shard_map/ppermute | solution.py:20
  63.7 17.1 %copy-start.98 = (pred[512,4]{0,1:T(4,128)(4,1)}, pred[512,4]{0,1:T(4,128)(4,1)S(1)}, u32[]{:S(2)}) copy-start(pred[512,4]{0,1:T(4,128)(4,1)S(1)} %broadcast_in_dim.502) | copy-start | bytes 6148
  67.9 12.9 %copy-start.101 = (pred[512,4]{0,1:T(4,128)(4,1)}, pred[512,4]{0,1:T(4,128)(4,1)S(1)}, u32[]{:S(2)}) copy-start(pred[512,4]{0,1:T(4,128)(4,1)S(1)} %broadcast_in_dim.486) | copy-start | bytes 6148
  74.9 18.1 %copy-start.60 = (bf16[128,2,4,48]{0,3,2,1:T(8,128)(2,1)S(1)}, bf16[128,2,4,48]{0,3,2,1:T(8,128)(2,1)}, u32[]{:S(2)}) copy-start(bf16[128,2,4,48]{0,3,2,1:T(8,128)(2,1)} %fusion.180) | copy-start | bytes 294916
  78.6 4.5 collective-permute-start.8
  82.0 3.6 collective-permute-start.3
  83.2 4.9 collective-permute-start.9
  85.7 8.4 %collective-permute-start.4 = (bf16[128,384]{0,1:T(8,128)(2,1)S(1)}, bf16[128,384]{0,1:T(8,128)(2,1)S(1)}, u32[]{:S(2)}, u32[]{:S(2)}) collective-permute-start(bf16[128,384]{0,1:T(8,128)(2,1)S(1)} %maximum_select_fusion.12), channel_id=1, source_target_pairs={{0,16},{16,0},{4,20},{20,4},{8,24},{24,8},{12,28},{28,12},{32,48},... | collective-permute-start | bytes 294920 | tf_op jit(solution)/shard_map/ppermute | solution.py:20
  88.2 8.8 %collective-permute-start.10 = (bf16[128,384]{1,0:T(8,128)(2,1)S(1)}, bf16[128,384]{1,0:T(8,128)(2,1)S(1)}, u32[]{:S(2)}, u32[]{:S(2)}) collective-permute-start(bf16[128,384]{1,0:T(8,128)(2,1)S(1)} %maximum_select_fusion.15), channel_id=1, source_target_pairs={{0,64},{64,0},{4,68},{68,4},{8,72},{72,8},{12,76},{76,12},{16,80},... | collective-permute-start | bytes 294920 | tf_op jit(solution)/shard_map/ppermute | solution.py:20
  92.3 10.2 %collective-permute-start.1 = (bf16[256,384]{0,1:T(8,128)(2,1)}, bf16[256,384]{0,1:T(8,128)(2,1)}, u32[]{:S(2)}, u32[]{:S(2)}) collective-permute-start(bf16[256,384]{0,1:T(8,128)(2,1)} %maximum_select_fusion.4), channel_id=1, source_target_pairs={{0,8},{8,0},{4,12},{12,4},{16,24},{24,16},{20,28},{28,20},{32,40},... | collective-permute-start | bytes 589832 | tf_op jit(solution)/shard_map/ppermute | solution.py:20
  94.8 19.3 %collective-permute-start.5 = (bf16[256,384]{0,1:T(8,128)(2,1)}, bf16[256,384]{0,1:T(8,128)(2,1)}, u32[]{:S(2)}, u32[]{:S(2)}) collective-permute-start(bf16[256,384]{0,1:T(8,128)(2,1)} %maximum_select_fusion.6), channel_id=1, source_target_pairs={{0,32},{32,0},{4,36},{36,4},{8,40},{40,8},{12,44},{44,12},{16,48},... | collective-permute-start | bytes 589832 | tf_op jit(solution)/shard_map/ppermute | solution.py:20
  97.7 21.9 %collective-permute-start.11 = (bf16[256,384]{1,0:T(8,128)(2,1)}, bf16[256,384]{1,0:T(8,128)(2,1)}, u32[]{:S(2)}, u32[]{:S(2)}) collective-permute-start(bf16[256,384]{1,0:T(8,128)(2,1)} %maximum_select_fusion.8), channel_id=1, source_target_pairs={{0,128},{128,0},{4,132},{132,4},{8,136},{136,8},{12,140},{140,12},... | collective-permute-start | bytes 589832 | tf_op jit(solution)/shard_map/ppermute | solution.py:20
  124.4 7.3 %copy-start.28 = (f32[128,4,4]{1,0,2:T(8,128)S(1)}, f32[128,4,4]{1,0,2:T(8,128)}, u32[]{:S(2)}) copy-start(f32[128,4,4]{1,0,2:T(8,128)} %reshape.1247) | copy-start | bytes 24580
  129.6 10.1 %copy-start.72 = (f32[4,32,512]{2,1,0:T(8,128)S(1)}, f32[4,32,512]{2,1,0:T(8,128)}, u32[]{:S(2)}) copy-start(f32[4,32,512]{2,1,0:T(8,128)} %copy-done.71) | copy-start | bytes 786436
  134.3 8.3 %copy-start.35 = (bf16[512,2,4,48]{0,3,2,1:T(8,128)(2,1)S(1)}, bf16[512,2,4,48]{0,3,2,1:T(8,128)(2,1)}, u32[]{:S(2)}) copy-start(bf16[512,2,4,48]{0,3,2,1:T(8,128)(2,1)} %copy-done.34) | copy-start | bytes 1179652
  150.6 11.1 %copy-start.8 = (f32[512,1,4,48]{0,3,2,1:T(8,128)}, f32[512,1,4,48]{0,3,2,1:T(8,128)S(1)}, u32[]{:S(2)}) copy-start(f32[512,1,4,48]{0,3,2,1:T(8,128)S(1)} %convolution_bitcast_fusion) | copy-start | bytes 1179652
  152.5 9.1 %copy-start.10 = (f32[512,1,4,48]{0,3,2,1:T(8,128)}, f32[512,1,4,48]{0,3,2,1:T(8,128)S(1)}, u32[]{:S(2)}) copy-start(f32[512,1,4,48]{0,3,2,1:T(8,128)S(1)} %fusion.26) | copy-start | bytes 1179652
  160.9 32.1 %collective-permute-start.14 = (bf16[256,384]{0,1:T(8,128)(2,1)}, bf16[256,384]{0,1:T(8,128)(2,1)}, u32[]{:S(2)}, u32[]{:S(2)}) collective-permute-start(bf16[256,384]{0,1:T(8,128)(2,1)} %bitcast.179), channel_id=1, source_target_pairs={{0,32},{32,0},{4,36},{36,4},{8,40},{40,8},{12,44},{44,12},{16,48},... | collective-permute-start | bytes 589832 | tf_op jit(solution)/shard_map/ppermute | solution.py:20
  162.4 34.5 %collective-permute-start.18 = (bf16[256,384]{0,1:T(8,128)(2,1)}, bf16[256,384]{0,1:T(8,128)(2,1)}, u32[]{:S(2)}, u32[]{:S(2)}) collective-permute-start(bf16[256,384]{0,1:T(8,128)(2,1)} %bitcast.190), channel_id=1, source_target_pairs={{0,128},{128,0},{4,132},{132,4},{8,136},{136,8},{12,140},{140,12},... | collective-permute-start | bytes 589832 | tf_op jit(solution)/shard_map/ppermute | solution.py:20
  171.3 27.3 %collective-permute-start.12 = (bf16[256,384]{0,1:T(8,128)(2,1)}, bf16[256,384]{0,1:T(8,128)(2,1)}, u32[]{:S(2)}, u32[]{:S(2)}) collective-permute-start(bf16[256,384]{0,1:T(8,128)(2,1)} %bitcast.168), channel_id=1, source_target_pairs={{0,8},{8,0},{4,12},{12,4},{16,24},{24,16},{20,28},{28,20},{32,40},... | collective-permute-start | bytes 589832 | tf_op jit(solution)/shard_map/ppermute | solution.py:20
  194.9 9.2 %collective-permute-start.15 = (bf16[128,384]{0,1:T(8,128)(2,1)S(1)}, bf16[128,384]{0,1:T(8,128)(2,1)S(1)}, u32[]{:S(2)}, u32[]{:S(2)}) collective-permute-start(bf16[128,384]{0,1:T(8,128)(2,1)S(1)} %select_convert_fusion.10), channel_id=1, source_target_pairs={{0,16},{16,0},{4,20},{20,4},{8,24},{24,8},{12,28},{28,12},{32,48},... | collective-permute-start | bytes 294920 | tf_op jit(solution)/shard_map/ppermute | solution.py:20
  197.9 7.1 %collective-permute-start.19 = (bf16[128,384]{0,1:T(8,128)(2,1)S(1)}, bf16[128,384]{0,1:T(8,128)(2,1)S(1)}, u32[]{:S(2)}, u32[]{:S(2)}) collective-permute-start(bf16[128,384]{0,1:T(8,128)(2,1)S(1)} %select_convert_fusion.7), channel_id=1, source_target_pairs={{0,64},{64,0},{4,68},{68,4},{8,72},{72,8},{12,76},{76,12},{16,80},... | collective-permute-start | bytes 294920 | tf_op jit(solution)/shard_map/ppermute | solution.py:20
  199.7 7.7 %collective-permute-start.13 = (bf16[128,384]{0,1:T(8,128)(2,1)S(1)}, bf16[128,384]{0,1:T(8,128)(2,1)S(1)}, u32[]{:S(2)}, u32[]{:S(2)}) collective-permute-start(bf16[128,384]{0,1:T(8,128)(2,1)S(1)} %select_convert_fusion.11), channel_id=1, source_target_pairs={{0,4},{4,0},{8,12},{12,8},{16,20},{20,16},{24,28},{28,24},{32,36},... | collective-permute-start | bytes 294920 | tf_op jit(solution)/shard_map/ppermute | solution.py:20
  204.8 12.6 %collective-permute-start.16 = (bf16[64,384]{0,1:T(8,128)(2,1)}, bf16[64,384]{0,1:T(8,128)(2,1)}, u32[]{:S(2)}, u32[]{:S(2)}) collective-permute-start(bf16[64,384]{0,1:T(8,128)(2,1)} %select_convert_fusion.9), channel_id=1, source_target_pairs={{0,8},{8,0},{4,12},{12,4},{16,24},{24,16},{20,28},{28,20},{32,40},... | collective-permute-start | bytes 147464 | tf_op jit(solution)/shard_map/ppermute | solution.py:20
  206.4 7.0 %collective-permute-start.20 = (bf16[64,384]{0,1:T(8,128)(2,1)}, bf16[64,384]{0,1:T(8,128)(2,1)}, u32[]{:S(2)}, u32[]{:S(2)}) collective-permute-start(bf16[64,384]{0,1:T(8,128)(2,1)} %select_convert_fusion.6), channel_id=1, source_target_pairs={{0,32},{32,0},{4,36},{36,4},{8,40},{40,8},{12,44},{44,12},{16,48},... | collective-permute-start | bytes 147464 | tf_op jit(solution)/shard_map/ppermute | solution.py:20
  214.8 6.1 %collective-permute-start.21 = (bf16[32,384]{0,1:T(8,128)(2,1)S(1)}, bf16[32,384]{0,1:T(8,128)(2,1)S(1)}, u32[]{:S(2)}, u32[]{:S(2)}) collective-permute-start(bf16[32,384]{0,1:T(8,128)(2,1)S(1)} %select_convert_fusion.5), channel_id=1, source_target_pairs={{0,16},{16,0},{4,20},{20,4},{8,24},{24,8},{12,28},{28,12},{32,48},... | collective-permute-start | bytes 73736 | tf_op jit(solution)/shard_map/ppermute | solution.py:20
  218.6 3.6 collective-permute-start.17
  221.1 3.6 collective-permute-start.22
  225.6 10.3 %collective-permute-start.23 = (bf16[8,384]{0,1:T(8,128)(2,1)}, bf16[8,384]{0,1:T(8,128)(2,1)}, u32[]{:S(2)}, u32[]{:S(2)}) collective-permute-start(bf16[8,384]{0,1:T(8,128)(2,1)} %select_convert_fusion.3), channel_id=1, source_target_pairs={{0,4},{4,0},{8,12},{12,8},{16,20},{20,16},{24,28},{28,24},{32,36},... | collective-permute-start | bytes 18440 | tf_op jit(solution)/shard_map/ppermute | solution.py:20
  245.8 246.8 %all-reduce.7.cloned.1.call-start = ((), (), s32[]{:S(2)}) async-start(), calls=%async_computation.1 | async-start | bytes 3145728 | tf_op jit(solution)/shard_map/psum | solution.py:247
  438.3 56.3 %copy-start.128 = (s32[512]{0:T(512)S(1)}, s32[512]{0:T(512)}, u32[]{:S(2)}) copy-start(s32[512]{0:T(512)} %copy-done.126) | copy-start | bytes 6148
  (116 other events, 368.6 us)
Sparse Core Ops, SparseCore 0:
  245.9 187.5 all-reduce.4
  436.5 56.0 all-reduce.6
where the time goes:
time: 512 us; the launch traced here: 505 us
  waiting for transfers between devices  241 us (47%)
  local copies, waits for them, and re-layouts  104 us (20%)
  other arithmetic  51.7 us (10%)
  matrix products  50.7 us (10%)
  starting transfers between devices  40.3 us (8%)
  between operations  17.1 us (3%)
    psum x1, waiting for transfers between devices, shards(): summed_qkv, summed_out = lax.psum((term_qkv, term_out), 'seq')  184 us
    psum x1, waiting for transfers between devices, shards(): lax.psum(jnp.dot(heads_flat, w_out, preferred_element_type=jnp.float32).a...  54.3 us
    broadcast_in_dim x66, local copies, waits for them, and re-layouts, spread_heads(): jnp.where(chosen.reshape(shape), selected[:, None], jnp.zeros((), selecte...  42.9 us
    ppermute x24, starting transfers between devices, swapped(): return lax.ppermute(block, axis, route)  40.2 us
    dynamic_slice x62, local copies, waits for them, and re-layouts, pick_heads(): lax.dynamic_index_in_dim(shaped[:, :, head_index], offsets[head_index], 1...  29.6 us
    select_n x19, other arithmetic, collect_swaps(): jnp.where(upper_bit == 0, jnp.concatenate([gathered, partner], 0), jnp.co...  11.2 us
    unnamed x284, local copies, waits for them, and re-layouts  10.8 us
  transfers between devices with their start and end apart: 26, of which 4 were waited for; matrix products, arithmetic and copies ran while one was open for 27% of the time, Pallas kernels for 0%

commit v1 on v0

v1 whole, which is shorter than its diff:
```python
import jax
import jax.numpy as jnp
from jax import lax
from jax.experimental import pallas as pl
from jax.experimental.pallas import tpu as pltpu
from jax.sharding import PartitionSpec as P

BF = jnp.bfloat16
F32 = jnp.float32
I32 = jnp.int32
T = 512
D = 768
HD = 48
C = 4 * HD
DROP = 1024.0 / 922.0
FACTOR = HD**-0.5
C1 = FACTOR * 1.4426950408889634
NEG = -1e30


def nt(a, b):
    return lax.dot_general(a, b, (((1,), (1,)), ((), ())), preferred_element_type=F32)


def nn(a, b):
    return lax.dot_general(a, b, (((1,), (0,)), ((), ())), preferred_element_type=F32)


def rows(n, m=1):
    return lax.broadcasted_iota(I32, (n, m), 0)


def lanes(m, n=1):
    return lax.broadcasted_iota(I32, (n, m), 1)


def head_of(x, top):
    total = jnp.zeros_like(x)
    for j in range(1, top):
        total = total + (x >= j * HD).astype(I32)
    return total


def lane_mask(c):
    col = lanes(C)
    return jnp.where((col >= c * HD) & (col < (c + 1) * HD), 1.0, 0.0)


def slide(pos, len_ref):
    e0 = len_ref[0]
    e1 = e0 + len_ref[1]
    e2 = e1 + len_ref[2]
    return (pos >= e0).astype(I32) + (pos >= e1).astype(I32) + (pos >= e2).astype(I32)


def bias_of(a, b):
    return jnp.where(a == b, 0.0, NEG)


def keep(salt, first, n):
    index = (first + rows(n, D)) * D + lanes(D, n)
    mixed = index * 747796405 + salt
    mixed = mixed ^ (mixed >> 13)
    mixed = mixed * 1274126177
    mixed = mixed ^ (mixed >> 16)
    return (mixed & 1023) >= 102


def standard(x):
    wide = x.astype(F32)
    centred = wide - jnp.mean(wide, -1, keepdims=True)
    inv = lax.rsqrt(jnp.mean(centred * centred, -1, keepdims=True) + 1e-05)
    return centred * inv, inv


def off_near(s):
    return ((s & 1) << 1) | (s >> 1)


def off_mid(s):
    return ((s & 1) << 3) | (s & 6) | (s >> 3)


def off_far(s):
    return ((s & 1) << 5) | ((s & 2) << 3) | ((s & 4) << 1) | ((s >> 2) & 6) | (s >> 5)


def base_near(r, place):
    return (place ^ off_near(r >> 7)) * T + (r & 127) * 4


def base_mid(r, place):
    return (place ^ off_mid(r >> 5)) * T + (r & 31) * 16


def base_far(r, place):
    return (place ^ off_far(r >> 3)) * T + (r & 7) * 64


def route_near():
    return jnp.where((lanes(T, 128) >> 2) == rows(128, T), 1.0, 0.0).astype(BF)


def route_mid():
    return jnp.where((lanes(T, 128) >> 4) == (rows(128, T) & 31), 1.0, 0.0).astype(BF)


def route_far():
    r = rows(128, T)
    return jnp.where(((lanes(T, 128) >> 6) == (r & 7)) & (r < 32), 1.0, 0.0).astype(BF)


def spread(a, route, ok):
    half = a * 0.5
    hi = half.astype(BF)
    lo = (half - hi.astype(F32)).astype(BF)
    out = (nn(hi, route) + nn(lo, route)) * 2.0
    return jnp.where(ok, out, 0.0)


def row_head(n):
    r = rows(n)
    h = head_of(jnp.minimum(r, C - 1), 4)
    return jnp.where(r < C, h, (r - C) >> 3)


def turned(x):
    return jnp.transpose(x.astype(F32)).astype(BF)


def branch_kernel(idx, salt, cot, branch):
    drop = jnp.where(keep(salt[0], idx[0] * T, T), DROP, 0.0)
    branch[...] = (cot[...].astype(F32) * drop).astype(BF)


def start_kernel(idx, tiles, w, w_out, branch, x_ref, near, mid, far, normed_ref):
    member = idx[1]
    xhat, _ = standard(tiles[...])
    normed = xhat.astype(BF)
    normed_ref[...] = normed
    x_ref[:, : 3 * C] = nt(normed, w[...]).astype(BF)
    x_ref[:, 3 * C :] = nt(branch[...], w_out[...]).astype(BF)
    x = x_ref[...].astype(F32)
    lane_head = head_of(lanes(D), 16) & 3
    p = rows(T)
    for out, count, rate, shift in ((near, 128, 4, 2), (mid, 32, 16, 4), (far, 8, 64, 6)):
        first = (4 * member) & (rate - 1)
        chosen = jnp.where((p & (rate - 1)) == first + lane_head, x, 0.0).astype(BF)
        n = max(count, 16)
        pick = jnp.where((lanes(T, n) >> shift) == rows(n, T), 1.0, 0.0).astype(BF)
        out[...] = nn(pick, chosen)[:count].astype(BF)


def local_stats_kernel(idx, lens, x_ref, st, vt, bias):
    place = idx[0]
    first = place * T
    q = x_ref[:, :C]
    k = x_ref[:, C : 2 * C]
    vt[...] = turned(x_ref[:, 2 * C : 3 * C])
    bias[...] = bias_of(slide(first + rows(T), lens), slide(first + lanes(T), lens))

    def step(c, carry):
        qc = q * lane_mask(c).astype(BF)
        w = jnp.exp2(nt(k, qc) * C1 + bias[...])
        top = pl.multiple_of(c * HD, 16)
        st[pl.ds(top, HD), :] = nn(vt[pl.ds(top, HD), :], w.astype(BF))
        st[pl.ds(pl.multiple_of(C + 8 * c, 8), 8), :] = jnp.broadcast_to(
            jnp.sum(w, 0, keepdims=True), (8, T)
        )
        return carry

    lax.fori_loop(0, 4, step, 0)


def near_stats_kernel(idx, lens, n0, n1, st, vt):
    place = idx[0]
    k = jnp.concatenate([n0[:, C : 2 * C], n1[:, C : 2 * C]], 0)
    vt[...] = turned(jnp.concatenate([n0[:, 2 * C : 3 * C], n1[:, 2 * C : 3 * C]], 0))
    q = n0[:128, :C]

    def step(c, carry):
        qc = q * lane_mask(c).astype(BF)
        bias = bias_of(
            slide(base_near(rows(T), place) + c, lens),
            slide(place * T + lanes(128) * 4 + c, lens),
        )
        w = jnp.exp2(nt(k, qc) * C1 + bias)
        top = pl.multiple_of(c * HD, 16)
        st[pl.ds(top, HD), :] = nn(vt[pl.ds(top, HD), :], w.astype(BF))
        st[pl.ds(pl.multiple_of(C + 8 * c, 8), 8), :] = jnp.broadcast_to(
            jnp.sum(w, 0, keepdims=True), (8, 128)
        )
        return carry

    lax.fori_loop(0, 4, step, 0)


def stacked(own, count):
    wide = own.astype(F32)
    parts = [wide * lane_mask(c) for c in range(4)]
    if count * 4 < 128:
        parts.append(jnp.zeros((128 - 4 * count, C), F32))
    return jnp.concatenate(parts, 0).astype(BF)


def wide_bias(base, count, rate, member, place, lens):
    shift = count.bit_length() - 1
    off = ((4 * member) & (rate - 1)) + (lanes(128) >> shift)
    q_pos = place * T + (lanes(128) & (count - 1)) * rate + off
    k_pos = base + off
    return bias_of(slide(k_pos, lens), slide(q_pos, lens))


def far_count(level):
    return (32, 16, base_mid) if level == 0 else (8, 64, base_far)


def half_pair(g0, g1, level, a, b):
    lo = 256 * level
    return jnp.concatenate([g0[lo : lo + 256, a:b], g1[lo : lo + 256, a:b]], 0)


def split3(x):
    hi = x.astype(BF).astype(F32)
    mid = (x - hi).astype(BF).astype(F32)
    lo = (x - hi - mid).astype(BF).astype(F32)
    return hi, mid, lo


def combine_kernel(idx, lens, x_ref, st_local, st_near, g0, g1, w_out, p0, p1, p2, p3, heads_t, full, own, aux_n, aux_m, aux_f, acc, heads):
    place, member = idx[0], idx[1]
    p = lanes(T)
    rh = row_head(C + 32)
    acc[...] = st_local[...] + spread(st_near[...], route_near(), (p & 3) == rh)
    for level in range(2):
        count, rate, base = far_count(level)
        shift = count.bit_length() - 1
        lo = 256 * level
        k = half_pair(g0, g1, level, C, 2 * C)
        vt = turned(half_pair(g0, g1, level, 2 * C, 3 * C))
        qbd = stacked(g0[lo : lo + max(count, 16), :C][:count], count)
        bias = wide_bias(base(rows(T), place), count, rate, member, place, lens)
        w = jnp.exp2(nt(k, qbd) * C1 + bias)
        lane_head = lanes(128) >> shift
        numer = nn(vt, w.astype(BF))
        totals = jnp.broadcast_to(jnp.sum(w, 0, keepdims=True), (32, 128))
        both = jnp.where(rh == lane_head, jnp.concatenate([numer, totals], 0), 0.0)
        route = route_mid() if level == 0 else route_far()
        ok = (p & (rate - 1)) == ((4 * member) & (rate - 1)) + rh
        acc[...] = acc[...] + spread(both, route, ok)
    gt = jnp.transpose(x_ref[:, 3 * C :].astype(F32))
    r8 = rows(8)
    pieces, mixes = [], []
    for c in range(4):
        total = acc[C + 8 * c : C + 8 * c + 1, :]
        mixed = acc[HD * c : HD * (c + 1), :] / total
        delta = jnp.sum(gt[HD * c : HD * (c + 1), :] * mixed, 0, keepdims=True)
        mixes.append(mixed)
        piece = jnp.zeros((8, T), F32)
        for j, part in enumerate(split3(jnp.log2(total)) + split3(delta)):
            piece = jnp.where(r8 == j, part, piece)
        pieces.append(piece)
    mixed = jnp.concatenate(mixes, 0)
    heads_t[...] = mixed.astype(BF)
    heads[...] = jnp.transpose(mixed).astype(BF)
    for j, out in enumerate((p0, p1, p2, p3)):
        at = pl.ds(pl.multiple_of((member ^ j) * 128, 128), 128)
        out[...] = nn(heads[at, :], w_out[...]).astype(BF)
    a32 = jnp.concatenate(pieces, 0)
    full[...] = a32
    rh32 = rows(32) >> 3
    for i, (rate, route, out, count) in enumerate(
        (
            (4, route_near(), aux_n, 128),
            (16, route_mid(), aux_m, 32),
            (64, route_far(), aux_f, 8),
        )
    ):
        ok = (p & (rate - 1)) == ((4 * member) & (rate - 1)) + rh32
        picked = nt(jnp.where(ok, a32, 0.0).astype(BF), route)
        own[32 * i : 32 * (i + 1), :] = picked
        square = jnp.concatenate([picked, jnp.zeros((96, 128), F32)], 0)
        out[...] = jnp.transpose(square)[:count].astype(BF)


def lse_of(a, c):
    return a[8 * c : 8 * c + 1] + a[8 * c + 1 : 8 * c + 2] + a[8 * c + 2 : 8 * c + 3]


def delta_of(a, c):
    return a[8 * c + 3 : 8 * c + 4] + a[8 * c + 4 : 8 * c + 5] + a[8 * c + 5 : 8 * c + 6]


def local_grads_kernel(idx, lens, x_ref, full, gqt, kv_ref, kt, bias, rowv):
    first = idx[0] * T
    q = x_ref[:, :C]
    k = x_ref[:, C : 2 * C]
    v = x_ref[:, 2 * C : 3 * C]
    g = x_ref[:, 3 * C :]
    kt[...] = turned(k)
    bias[...] = bias_of(slide(first + rows(T), lens), slide(first + lanes(T), lens))
    a = full[...]
    for c in range(4):
        rowv[c, 0:1, :] = lse_of(a, c)
        rowv[c, 1:2, :] = delta_of(a, c)
    kv_ref[...] = jnp.zeros((T, 2 * C), F32)

    def step(c, carry):
        m = lane_mask(c)
        mb = m.astype(BF)
        top = pl.multiple_of(c * HD, 16)
        w = jnp.exp2(nt(k, q * mb) * C1 + bias[...] - rowv[c, 0:1, :])
        low = w.astype(BF)
        ds = (w * (nt(v, g * mb) - rowv[c, 1:2, :])).astype(BF)
        kv_ref[:, :C] = kv_ref[:, :C] + nn(ds, q) * (m * FACTOR)
        kv_ref[:, C:] = kv_ref[:, C:] + nn(low, g) * m
        gqt[pl.ds(top, HD), :] = nn(kt[pl.ds(top, HD), :], ds)
        return carry

    lax.fori_loop(0, 4, step, 0)


def pack(keep_ref, send_ref, mine, parts):
    for j in range(8):
        block = mine ^ j
        out = keep_ref if j % 2 == 0 else send_ref
        lo = 96 * (j // 2)
        picked = [p[pl.ds(pl.multiple_of(block * n, 8), n), :] for p, n in parts]
        out[lo : lo + 96, :] = jnp.concatenate(picked, 0).astype(BF)


def query_grads_kernel(
    idx, lens, n0, n1, g0, g1, own, gqt, heads_t, branch, normed,
    gq_ref, term_q, term_out, kt, rowv, near_t,
):
    place, member = idx[0], idx[1]
    first = place * T
    o = own[...]
    for c in range(4):
        rowv[c, 2:3, 0:128] = lse_of(o[:32], c)
        rowv[c, 3:4, 0:128] = delta_of(o[:32], c)
    kn = jnp.concatenate([n0[:, C : 2 * C], n1[:, C : 2 * C]], 0)
    vn = jnp.concatenate([n0[:, 2 * C : 3 * C], n1[:, 2 * C : 3 * C]], 0)
    kt[...] = turned(kn)
    qn = n0[:128, :C]
    gn = n0[:128, 3 * C :]

    def near_step(c, carry):
        mb = lane_mask(c).astype(BF)
        top = pl.multiple_of(c * HD, 16)
        b = bias_of(
            slide(base_near(rows(T), place) + c, lens),
            slide(first + lanes(128) * 4 + c, lens),
        )
        w = jnp.exp2(nt(kn, qn * mb) * C1 + b - rowv[c, 2:3, 0:128])
        ds = (w * (nt(vn, gn * mb) - rowv[c, 3:4, 0:128])).astype(BF)
        near_t[pl.ds(top, HD), :] = nn(kt[pl.ds(top, HD), :], ds)
        return carry

    lax.fori_loop(0, 4, near_step, 0)
    p = lanes(T)
    rh = row_head(C)
    total = gqt[...] + spread(near_t[...], route_near(), (p & 3) == rh)
    for level in range(2):
        count, rate, base = far_count(level)
        shift = count.bit_length() - 1
        lo = 256 * level
        kk = half_pair(g0, g1, level, C, 2 * C)
        vv = half_pair(g0, g1, level, 2 * C, 3 * C)
        qbd = stacked(g0[lo : lo + max(count, 16), :C][:count], count)
        gbd = stacked(g0[lo : lo + max(count, 16), 3 * C :][:count], count)
        b = wide_bias(base(rows(T), place), count, rate, member, place, lens)
        lane_head = lanes(128) >> shift
        ol = o[32 + 32 * level : 64 + 32 * level]
        lse = jnp.zeros((1, 128), F32)
        delta = jnp.zeros((1, 128), F32)
        for c in range(4):
            lse = jnp.where(lane_head == c, lse_of(ol, c), lse)
            delta = jnp.where(lane_head == c, delta_of(ol, c), delta)
        w = jnp.where(lane_head < 4, jnp.exp2(nt(kk, qbd) * C1 + b - lse), 0.0)
        ds = (w * (nt(vv, gbd) - delta)).astype(BF)
        part = jnp.where(rh == lane_head, nn(turned(kk), ds), 0.0)
        route = route_mid() if level == 0 else route_far()
        ok = (p & (rate - 1)) == ((4 * member) & (rate - 1)) + rh
        total = total + spread(part, route, ok)
    total = total * FACTOR
    gq_ref[...] = jnp.transpose(total).astype(BF)
    term_out[...] = nn(heads_t[...], branch[...])
    term_q[...] = nn(total.astype(BF), normed[...])


def key_grads_kernel(
    idx, lens, n0, n1, g0, g1, a0, a1, kv, normed, term_q, term_out,
    gkv_ref, keep_ref, send_ref, rowv, sel, term,
):
    place, member = idx[0], idx[1]

    def aux_rows(level):
        lo = 256 * level
        both = jnp.concatenate([a0[lo : lo + 256, :], a1[lo : lo + 256, :]], 0)
        return jnp.transpose(both.astype(F32))

    near = aux_rows(0)
    for c in range(4):
        rowv[c, 0:1, :] = lse_of(near, c)
        rowv[c, 1:2, :] = delta_of(near, c)
    qn = jnp.concatenate([n0[:, :C], n1[:, :C]], 0)
    gn = jnp.concatenate([n0[:, 3 * C :], n1[:, 3 * C :]], 0)
    kn = n0[:128, C : 2 * C]
    vn = n0[:128, 2 * C : 3 * C]
    sel[...] = jnp.zeros((128, 2 * C), F32)

    def near_step(c, carry):
        m = lane_mask(c)
        mb = m.astype(BF)
        b = bias_of(
            slide(place * T + rows(128) * 4 + c, lens),
            slide(base_near(lanes(T), place) + c, lens),
        )
        w = jnp.exp2(nt(kn * mb, qn) * C1 + b - rowv[c, 0:1, :])
        low = w.astype(BF)
        ds = (w * (nt(vn * mb, gn) - rowv[c, 1:2, :])).astype(BF)
        sel[:, :C] = sel[:, :C] + nn(ds, qn) * m
        sel[:, C:] = sel[:, C:] + nn(low, gn) * m
        return carry

    lax.fori_loop(0, 4, near_step, 0)
    p = rows(T)
    lane_head8 = head_of(lanes(2 * C), 8) & 3
    scale = jnp.where(lanes(2 * C) < C, FACTOR, 1.0)

    def place_rows(x, rate, shift, count):
        take = jnp.where((rows(T, count) >> shift) == lanes(count, T), 1.0, 0.0).astype(BF)
        hi = x.astype(BF)
        lo = (x - hi.astype(F32)).astype(BF)
        ok = (p & (rate - 1)) == ((4 * member) & (rate - 1)) + lane_head8
        return jnp.where(ok, nn(take, hi) + nn(take, lo), 0.0)

    total = place_rows(sel[...], 4, 2, 128)
    for level in range(2):
        count, rate, base = far_count(level)
        shift = count.bit_length() - 1
        lo = 256 * level
        q = half_pair(g0, g1, level, 0, C)
        g = half_pair(g0, g1, level, 3 * C, 4 * C)
        kbd = stacked(g0[lo : lo + max(count, 16), C : 2 * C][:count], count)
        vbd = stacked(g0[lo : lo + max(count, 16), 2 * C : 3 * C][:count], count)
        row_c = rows(128) >> shift
        off = ((4 * member) & (rate - 1)) + row_c
        b = bias_of(
            slide(place * T + (rows(128) & (count - 1)) * rate + off, lens),
            slide(base(lanes(T), place) + off, lens),
        )
        aux = aux_rows(level + 1)
        lse = jnp.zeros((1, T), F32)
        delta = jnp.zeros((1, T), F32)
        for c in range(4):
            lse = jnp.where(row_c == c, lse_of(aux, c), lse)
            delta = jnp.where(row_c == c, delta_of(aux, c), delta)
        w = jnp.where(row_c < 4, jnp.exp2(nt(kbd, q) * C1 + b - lse), 0.0)
        ds = (w * (nt(vbd, g) - delta)).astype(BF)
        both = jnp.concatenate([nn(ds, q), nn(w.astype(BF), g)], 1)
        both = jnp.where(row_c == lane_head8, both, 0.0)
        merged = both[:count]
        for c in range(1, 4):
            merged = merged + both[c * count : (c + 1) * count]
        total = total + place_rows(
            jnp.concatenate([merged, jnp.zeros((128 - count, 2 * C), F32)], 0), rate, 4 if level == 0 else 6, 128
        )
    gkv = kv[...] + total * scale
    gkv_ref[...] = gkv.astype(BF)
    term[...] = nn(turned(gkv), normed[...])
    pack(keep_ref, send_ref, place & 7, ((term_q, 24), (term_out, 24), (term, 48)))


def back_kernel(gq, gkv, w, out):
    out[...] = (nn(gq[...], w[:C, :]) + nn(gkv[...], w[C:, :])).astype(BF)


def layer_kernel(idx, salt, p0, p1, p2, p3, out):
    drop = jnp.where(keep(salt[0], idx[0] * T + idx[1] * 128, 128), DROP, 0.0)
    proj = p0[...].astype(F32) + p1[...].astype(F32) + p2[...].astype(F32) + p3[...].astype(F32)
    out[...] = (proj * drop).astype(BF)


def tile_kernel(idx, tiles, grad, out):
    at = pl.ds(pl.multiple_of(idx[1] * 128, 128), 128)
    xhat, inv = standard(tiles[at, :])
    g = grad[...].astype(F32)
    mean = jnp.mean(g, -1, keepdims=True)
    cross = jnp.mean(g * xhat, -1, keepdims=True)
    out[...] = (inv * (g - mean - xhat * cross)).astype(BF)


def join_kernel(idx, t0, t1, t2, t3, out):
    for j, t in enumerate((t0, t1, t2, t3)):
        out[pl.ds(pl.multiple_of((idx[1] ^ j) * 128, 128), 128), :] = t[...]


def finish_kernel(scale, idx, s0, s1, gw, go):
    mine = idx[0] & 7
    for j in range(8):
        block = mine ^ j
        lo = 96 * (j // 2)
        src = s0 if j % 2 == 0 else s1
        wide = src[lo : lo + 96, :].astype(F32) * scale
        at = pl.ds(pl.multiple_of(block * 24, 8), 24)
        gw[at, :] = wide[:24]
        go[at, :] = wide[24:48]
        gw[pl.ds(pl.multiple_of(C + block * 48, 16), 48), :] = wide[48:]


def call(kernel, n_scalar, args, outs, scratch=(), flops=0):
    specs = [pl.BlockSpec(memory_space=pltpu.SMEM)] * n_scalar
    specs += [pl.BlockSpec(memory_space=pltpu.VMEM)] * (len(args) - n_scalar)
    return pl.pallas_call(
        kernel,
        in_specs=specs,
        out_specs=[pl.BlockSpec(memory_space=pltpu.VMEM)] * len(outs),
        out_shape=[jax.ShapeDtypeStruct(s, d) for s, d in outs],
        scratch_shapes=[pltpu.VMEM(s, d) for s, d in scratch],
        compiler_params=pltpu.CompilerParams(vmem_limit_bytes=40 * 2**20),
        cost_estimate=pl.CostEstimate(flops=flops, bytes_accessed=flops // 200, transcendentals=0),
    )(*args)


def shards(tiles, w_qkv, w_out, slide_lengths, drop_salt, cotangent):
    member = lax.axis_index("mp")
    place = lax.axis_index("seq")
    groups = lax.axis_size("seq")
    idx = jnp.stack([place, member]).astype(I32)

    def swap(x, mask):
        return lax.ppermute(x, "seq", [(i, i ^ mask) for i in range(groups)])

    def across(x, mask):
        return lax.ppermute(x, "mp", [(i, i ^ mask) for i in range(4)])

    def tie(a, b):
        return lax.optimization_barrier((a, b))

    cat = jnp.concatenate
    us = 10**9
    w_t = w_qkv.T

    (branch,) = call(branch_kernel, 2, (idx, drop_salt, cotangent), [((T, D), BF)], flops=3 * us)
    x, near, mid, far, normed = call(
        start_kernel, 1, (idx, tiles, w_t, w_out, branch),
        [((T, D), BF), ((128, D), BF), ((32, D), BF), ((8, D), BF), ((T, D), BF)], flops=4 * us,
    )
    got = swap(far, 32)
    got_n = swap(near, 2)
    (st_local,) = call(
        local_stats_kernel, 2, (idx, slide_lengths, x),
        [((C + 32, T), F32)], [((C, T), BF), ((T, T), F32)], flops=5 * us,
    )
    got, st_local = tie(got, st_local)
    far = cat([far, got], 0)
    n0 = cat([near, got_n], 0)
    n1 = swap(n0, 1)
    far = cat([far, swap(far, 16)], 0)
    got = swap(cat([mid, far], 0), 8)
    (st_near,) = call(
        near_stats_kernel, 2, (idx, slide_lengths, n0, n1),
        [((C + 32, 128), F32)], [((C, T), BF)], flops=2 * us,
    )
    got, st_near = tie(got, st_near)
    both = cat([mid, got[:32], far, got[32:]], 0)
    got = [both, swap(both, 2), swap(both, 4), swap(both, 6)]
    g0 = cat([b[:64] for b in got] + [b[64:] for b in got], 0)
    g1 = swap(g0, 1)

    p0, p1, p2, p3, heads_t, full, own, aux_n, aux_m, aux_f = call(
        combine_kernel, 2, (idx, slide_lengths, x, st_local, st_near, g0, g1, w_out),
        [((128, D), BF)] * 4
        + [((C, T), BF), ((32, T), F32), ((96, 128), F32), ((128, 128), BF), ((32, 128), BF), ((8, 128), BF)],
        [((C + 32, T), F32), ((T, C), BF)], flops=4 * us,
    )
    def wide(a):
        return a.astype(F32)

    def cut(part):
        return [part[96 * i : 96 * (i + 1)] for i in range(4)]

    def x_swaps(pieces):
        return [swap(pieces[i], 2 * i) for i in range(1, 4)]

    def x_sum(pieces, got):
        return (wide(pieces[0]) + (wide(got[0]) + wide(got[1])) + wide(got[2])).astype(BF)

    def plus(part, got):
        return (wide(part) + wide(got)).astype(BF)

    got = swap(aux_f, 32)
    p_in = [across(p1, 1), across(p3, 3), across(p2, 2)]
    gqt, kv = call(
        local_grads_kernel, 2, (idx, slide_lengths, x, full),
        [((C, T), F32), ((T, 2 * C), F32)],
        [((C, T), BF), ((T, T), F32), ((4, 8, T), F32)], flops=6 * us,
    )
    got, gqt = tie(got, gqt)
    far = cat([aux_f, got], 0)
    got = swap(far, 16)
    query = call(
        query_grads_kernel, 2,
        (idx, slide_lengths, n0, n1, g0, g1, own, gqt, heads_t, branch, normed),
        [((T, C), BF), ((C, D), F32), ((C, D), F32)],
        [((C, T), BF), ((4, 8, T), F32), ((C, 128), F32)], flops=6 * us,
    )
    got, ((gq, term_q, term_out), p_in) = tie(got, (query, p_in))
    (l0,) = call(layer_kernel, 2, (idx, drop_salt, p0, *p_in), [((128, D), BF)], flops=us)
    l_in = [across(l0, 1), across(l0, 2), across(l0, 3)]
    far = cat([far, got], 0)
    got = swap(cat([aux_m, far], 0), 8)
    both = cat([aux_m, got[:32], far, got[32:]], 0)
    first = swap(cat([both, aux_n], 0), 2)
    got = [both, first[:128], swap(both, 4), swap(both, 6)]
    a0 = cat([aux_n, first[128:]] + [b[:64] for b in got] + [b[64:] for b in got], 0)
    a1 = swap(a0, 1)

    key = call(
        key_grads_kernel, 2,
        (idx, slide_lengths, n0, n1, g0, g1, a0, a1, kv, normed, term_q, term_out),
        [((T, 2 * C), BF), ((384, D), BF), ((384, D), BF)],
        [((4, 8, T), F32), ((128, 2 * C), F32), ((2 * C, D), F32)], flops=5 * us,
    )
    (gkv, kept, sent), l_in = tie(key, l_in)
    got = swap(sent, 1)
    (back,) = call(back_kernel, 0, (gq, gkv, w_t), [((T, D), BF)], flops=us)
    got, back = tie(got, back)
    back = lax.psum_scatter(back, "mp", scatter_dimension=0, tiled=True)
    part = cut(plus(kept, got))
    part = x_sum(part, x_swaps(part))
    got = swap(part, 8)
    (layer_out,) = call(join_kernel, 1, (idx, l0, *l_in), [((T, D), BF)], flops=us)
    got, layer_out = tie(got, layer_out)
    part = plus(part, got)
    got, back = tie(swap(part, 16), back)
    part = plus(part, got)
    got = swap(part, 32)
    part = plus(part, got)
    got = x_swaps([part] * 4)
    (t0,) = call(tile_kernel, 1, (idx, tiles, back), [((128, D), BF)], flops=us)
    got, t_in = tie(got, [across(t0, j) for j in range(1, 4)])
    s0 = cat([part] + got, 0)
    s1 = swap(s0, 1)
    (tile_gradient,) = call(join_kernel, 1, (idx, t0, *t_in), [((T, D), BF)], flops=us)
    s1, tile_gradient = tie(s1, tile_gradient)
    scale = (T * groups) ** -0.5

    def finish(*refs):
        finish_kernel(scale, *refs)

    grad_w_t, grad_w_out = call(
        finish, 1, (idx, s0, s1), [((3 * C, D), F32), ((C, D), F32)], flops=us
    )
    return (layer_out, tile_gradient, grad_w_t.T, grad_w_out)


def solution(mesh):
    placed = (P("seq", None), P(None, "mp"), P("mp", None), P(), P(), P("seq", None))
    return jax.shard_map(
        shards,
        mesh=mesh,
        in_specs=placed,
        out_specs=(P("seq", None), P("seq", None), P(None, "mp"), P("mp", None)),
        check_vma=False,
    )
```

time: 512 us -> 164 us (0.32); the launches traced: 505 us -> 164 us
  waiting for transfers between devices: 241 us -> 52.1 us
  local copies, waits for them, and re-layouts: 104 us -> 2.57 us
  other arithmetic: 51.7 us -> 0.47 us
  matrix products: 50.7 us -> 0 us
  Pallas kernels: 0 us -> 35.9 us
  starting transfers between devices: 40.3 us -> 57.4 us
    psum x2 -> x0, waiting for transfers between devices: 238 us -> none  [the longest x1 184 us: shards(): summed_qkv, summed_out = lax.psum((term_qkv, term_out), 'seq')]
    dot_general x34 -> x0, matrix products: 50.7 us -> none  [the longest x4 7.52 us: weights_of(): jnp.einsum('bqhd,bkhd->bhqk', queries, keys_in, preferred_element_type=jn...]
    ppermute x24 -> x36, waiting for transfers between devices: 2.81 us -> 52.1 us  [the longest x27 46.5 us: swap(): return lax.ppermute(x, 'seq', [(i, i ^ mask) for i in range(groups)])]
    broadcast_in_dim x66 -> x0, local copies, waits for them, and re-layouts: 42.9 us -> none  [spread_heads(): jnp.where(chosen.reshape(shape), selected[:, None], jnp.zeros((), selecte...]
    pallas_call x0 -> x14, Pallas kernels: none -> 35.9 us  [call(): pl.pallas_call(kernel, in_specs=specs, out_specs=[pl.BlockSpec(memory_spa...]
    dynamic_slice x62 -> x0, local copies, waits for them, and re-layouts: 29.6 us -> none  [pick_heads(): lax.dynamic_index_in_dim(shaped[:, :, head_index], offsets[head_index], 1...]
    ppermute x24 -> x36, starting transfers between devices: 40.2 us -> 57.3 us  [the longest x27 46.7 us: swap(): return lax.ppermute(x, 'seq', [(i, i ^ mask) for i in range(groups)])]
    select_n x23 -> x0, other arithmetic: 12.8 us -> none  [the longest x19 11.2 us: collect_swaps(): jnp.where(upper_bit == 0, jnp.concatenate([gathered, partner], 0), jnp.co...]
  transfers between devices with their start and end apart: 26 -> 37, of which waited for: 4 -> 20; matrix products, arithmetic and copies ran while one was open for 27% -> 0% of each run, Pallas kernels for 0% -> 17%
where the time goes in v1:
time: 164 us
  starting transfers between devices  57.4 us (35%)
  waiting for transfers between devices  52.1 us (32%)
  Pallas kernels  35.9 us (22%)
  between operations  15.1 us (9%)
  local copies, waits for them, and re-layouts  2.57 us (2%)
    ppermute x27, starting transfers between devices, swap(): return lax.ppermute(x, 'seq', [(i, i ^ mask) for i in range(groups)])  46.7 us
    ppermute x27, waiting for transfers between devices, swap(): return lax.ppermute(x, 'seq', [(i, i ^ mask) for i in range(groups)])  46.5 us
    pallas_call x14, Pallas kernels, call(): pl.pallas_call(kernel, in_specs=specs, out_specs=[pl.BlockSpec(memory_spa...  35.9 us
    ppermute x9, starting transfers between devices, across(): return lax.ppermute(x, 'mp', [(i, i ^ mask) for i in range(4)])  10.6 us
    ppermute x9, waiting for transfers between devices, across(): return lax.ppermute(x, 'mp', [(i, i ^ mask) for i in range(4)])  5.6 us
  transfers between devices with their start and end apart: 37, of which 20 were waited for; matrix products, arithmetic and copies ran while one was open for 0% of the time, Pallas kernels for 17%

profile of v1, /device:TPU:1, one launch (start us, length us, event | category | flops | bytes accessed | tf_op | source)
XLA Modules:
  0.0 163.5 jit_solution(13930178457258159140)
XLA Ops:
  9.1 1.3 shard_map.93.branch
  10.5 2.3 %shard_map.94 = (bf16[512,768]{1,0:T(8,128)(2,1)S(1)}, bf16[128,768]{1,0:T(8,128)(2,1)S(1)}, bf16[32,768]{1,0:T(8,128)(2,1)S(1)}, bf16[8,768]{1,0:T(8,128)(2,1)S(1)}, bf16[512,768]{1,0:T(8,128)(2,1)S(1)}) custom-call(s32[2]{0:T(128)S(1)} %pad_add_fusion.idx.refs_0_, bf16[512,768]{1,0:T(8,128)(2,1)S(1)} %copy-done.2, bf16[576,768]{1,0:T(8,128)(2,1)S(1)} %bitcast.4, ...), custom_call_target="tpu_custom_call" | custom-call | flops 4000000000 | bytes 20000000 | tf_op jit(solution)/shard_map/pallas_call | solution.py:516
  12.9 2.1 %collective-permute-start = (bf16[128,768]{1,0:T(8,128)(2,1)S(1)}, bf16[128,768]{1,0:T(8,128)(2,1)S(1)}, u32[]{:S(2)}, u32[]{:S(2)}) collective-permute-start(bf16[128,768]{1,0:T(8,128)(2,1)S(1)} %get-tuple-element.62), channel_id=1, source_target_pairs={{0,8},{4,12},{8,0},{12,4},{16,24},{20,28},{24,16},{28,20},{32,40},... | collective-permute-start | bytes 589832 | tf_op jit(solution)/shard_map/ppermute | solution.py:534
  14.9 6.9 %collective-permute-start.2 = (bf16[8,768]{1,0:T(8,128)(2,1)S(1)}, bf16[8,768]{1,0:T(8,128)(2,1)S(1)}, u32[]{:S(2)}, u32[]{:S(2)}) collective-permute-start(bf16[8,768]{1,0:T(8,128)(2,1)S(1)} %get-tuple-element.64), channel_id=1, source_target_pairs={{0,128},{4,132},{8,136},{12,140},{16,144},{20,148},{24,152},{28,15... | collective-permute-start | bytes 36872 | tf_op jit(solution)/shard_map/ppermute | solution.py:534
  21.9 1.3 collective-permute-start.1
  23.2 2.9 %shard_map.95.st_local = f32[224,512]{1,0:T(8,128)S(1)} custom-call(s32[2]{0:T(128)S(1)} %pad_add_fusion.idx.refs_0_, s32[4]{0:T(128)S(1)} %copy-done.5, bf16[512,768]{1,0:T(8,128)(2,1)S(1)} %get-tuple-element.65.x_ref), custom_call_target="tpu_custom_call" | custom-call | flops 5000000000 | bytes 25000000 | tf_op jit(solution)/shard_map/pallas_call | solution.py:516
  26.1 1.3 collective-permute-start.3
  27.4 2.4 %collective-permute-done.3 = bf16[16,768]{1,0:T(8,128)(2,1)S(1)} collective-permute-done((bf16[16,768]{1,0:T(8,128)(2,1)S(1)}, bf16[16,768]{1,0:T(8,128)(2,1)S(1)}, u32[]{:S(2)}, u32[]{:S(2)}) %collective-permute-start.3) | collective-permute-done | bytes 24608 | tf_op jit(solution)/shard_map/ppermute | solution.py:534
  30.6 2.6 %shard_map.96.st_near = f32[224,128]{1,0:T(8,128)S(1)} custom-call(s32[2]{0:T(128)S(1)} %pad_add_fusion.idx.refs_0_, s32[4]{0:T(128)S(1)} %copy-done.5, bf16[256,768]{1,0:T(8,128)(2,1)S(1)} %constant_dynamic-update-slice_fusion.n0, bf16[256,768]{1,0:T(8,128)(2,1)S(1)} %collective-permute-done.1.n1), custom_call_target="tpu_custom_call" | custom-call | flops 2000000000 | bytes 10000000 | tf_op jit(solution)/shard_map/pallas_call | solution.py:516
  34.4 1.8 %collective-permute-start.7 = (bf16[128,768]{1,0:T(8,128)(2,1)S(1)}, bf16[128,768]{1,0:T(8,128)(2,1)S(1)}, u32[]{:S(2)}, u32[]{:S(2)}) collective-permute-start(bf16[128,768]{1,0:T(8,128)(2,1)S(1)} %get-tuple-element.123), channel_id=1, source_target_pairs={{0,24},{4,28},{8,16},{12,20},{16,8},{20,12},{24,0},{28,4},{32,56},... | collective-permute-start | bytes 589832 | tf_op jit(solution)/shard_map/ppermute | solution.py:534
  36.7 1.3 collective-permute-done.5
  38.0 5.8 %collective-permute-done.6 = bf16[128,768]{1,0:T(8,128)(2,1)S(1)} collective-permute-done((bf16[128,768]{1,0:T(8,128)(2,1)S(1)}, bf16[128,768]{1,0:T(8,128)(2,1)S(1)}, u32[]{:S(2)}, u32[]{:S(2)}) %collective-permute-start.6) | collective-permute-done | bytes 196640 | tf_op jit(solution)/shard_map/ppermute | solution.py:534
  43.9 3.4 %collective-permute-start.8 = (bf16[512,768]{1,0:T(8,128)(2,1)S(1)}, bf16[512,768]{1,0:T(8,128)(2,1)S(1)}, u32[]{:S(2)}, u32[]{:S(2)}) collective-permute-start(bf16[512,768]{1,0:T(8,128)(2,1)S(1)} %slice_dynamic-update-slice_fusion.g0), channel_id=1, source_target_pairs={{0,4},{4,0},{8,12},{12,8},{16,20},{20,16},{24,28},{28,24},{32,36},... | collective-permute-start | bytes 2359304 | tf_op jit(solution)/shard_map/ppermute | solution.py:534
  47.4 1.9 %collective-permute-done.8.g1 = bf16[512,768]{1,0:T(8,128)(2,1)S(1)} collective-permute-done((bf16[512,768]{1,0:T(8,128)(2,1)S(1)}, bf16[512,768]{1,0:T(8,128)(2,1)S(1)}, u32[]{:S(2)}, u32[]{:S(2)}) %collective-permute-start.8) | collective-permute-done | bytes 786464 | tf_op jit(solution)/shard_map/ppermute | solution.py:534
  49.3 2.9 %shard_map.97 = (bf16[128,768]{1,0:T(8,128)(2,1)S(1)}, bf16[128,768]{1,0:T(8,128)(2,1)S(1)}, bf16[128,768]{1,0:T(8,128)(2,1)S(1)}, bf16[128,768]{1,0:T(8,128)(2,...) custom-call(s32[2]{0:T(128)S(1)} %pad_add_fusion.idx.refs_0_, ...), custom_call_target="tpu_custom_call" | custom-call | flops 4000000000 | bytes 20000000 | tf_op jit(solution)/shard_map/pallas_call | solution.py:516
  52.2 5.4 %collective-permute-start.9 = (bf16[8,128]{1,0:T(8,128)(2,1)S(1)}, bf16[8,128]{1,0:T(8,128)(2,1)S(1)}, u32[]{:S(2)}, u32[]{:S(2)}) collective-permute-start(bf16[8,128]{1,0:T(8,128)(2,1)S(1)} %get-tuple-element.72), channel_id=1, source_target_pairs={{0,128},{4,132},{8,136},{12,140},{16,144},{20,148},{24,152},{28,15... | collective-permute-start | bytes 6152 | tf_op jit(solution)/shard_map/ppermute | solution.py:534
  57.6 1.3 collective-permute-start.11
  58.9 1.9 %collective-permute-start.12 = (bf16[128,768]{1,0:T(8,128)(2,1)S(1)}, bf16[128,768]{1,0:T(8,128)(2,1)S(1)}, u32[]{:S(2)}, u32[]{:S(2)}) collective-permute-start(bf16[128,768]{1,0:T(8,128)(2,1)S(1)} %get-tuple-element.84), channel_id=1, source_target_pairs={{0,3},{1,2},{2,1},{3,0},{4,7},{5,6},{6,5},{7,4},{8,11},{9,10},{10,... | collective-permute-start | bytes 589832 | tf_op jit(solution)/shard_map/ppermute | solution.py:537
  61.5 4.8 %shard_map.98 = (f32[192,512]{1,0:T(8,128)S(1)}, f32[512,384]{1,0:T(8,128)S(1)}) custom-call(s32[2]{0:T(128)S(1)} %pad_add_fusion.idx.refs_0_, s32[4]{0:T(128)S(1)} %copy-done.5, bf16[512,768]{1,0:T(8,128)(2,1)S(1)} %get-tuple-element.65.x_ref, f32[32,512]{1,0:T(8,128)S(1)} %get-tuple-element.73.full), custom_call_target="tpu_custom_call" | custom-call | flops 6000000000 | bytes 30000000 | tf_op jit(solution)/shard_map/pallas_call | solution.py:516
  66.4 1.3 collective-permute-start.10
  67.7 5.3 %shard_map.99 = (bf16[512,192]{1,0:T(8,128)(2,1)S(1)}, f32[192,768]{1,0:T(8,128)S(1)}, f32[192,768]{1,0:T(8,128)S(1)}) custom-call(s32[2]{0:T(128)S(1)} %pad_add_fusion.idx.refs_0_, s32[4]{0:T(128)S(1)} %copy-done.5, bf16[256,768]{1,0:T(8,128)(2,1)S(1)} %constant_dynamic-update-slice_fusion.n0, bf16[256,768]{1,0:T(8,128)(2,1)S(1)} %collective-permute-done.1.n1, ...), custom_call_target="tpu_custom_call" | custom-call | flops 6000000000 | bytes 30000000 | tf_op jit(solution)/shard_map/pallas_call | solution.py:516
  73.8 1.9 %collective-permute-done.14 = bf16[64,128]{1,0:T(8,128)(2,1)S(1)} collective-permute-done((bf16[64,128]{1,0:T(8,128)(2,1)S(1)}, bf16[64,128]{1,0:T(8,128)(2,1)S(1)}, u32[]{:S(2)}, u32[]{:S(2)}) %collective-permute-start.14) | collective-permute-done | bytes 16416 | tf_op jit(solution)/shard_map/ppermute | solution.py:534
  75.9 3.1 %collective-permute-done.15 = bf16[256,128]{1,0:T(8,128)(2,1)S(1)} collective-permute-done((bf16[256,128]{1,0:T(8,128)(2,1)S(1)}, bf16[256,128]{1,0:T(8,128)(2,1)S(1)}, u32[]{:S(2)}, u32[]{:S(2)}) %collective-permute-start.15) | collective-permute-done | bytes 65568 | tf_op jit(solution)/shard_map/ppermute | solution.py:534
  79.0 1.6 collective-permute-start.17
  81.0 3.9 %collective-permute-done.16 = bf16[128,128]{1,0:T(8,128)(2,1)S(1)} collective-permute-done((bf16[128,128]{1,0:T(8,128)(2,1)S(1)}, bf16[128,128]{1,0:T(8,128)(2,1)S(1)}, u32[]{:S(2)}, u32[]{:S(2)}) %collective-permute-start.16) | collective-permute-done | bytes 32800 | tf_op jit(solution)/shard_map/ppermute | solution.py:534
  85.0 5.3 %collective-permute-start.18 = (bf16[768,128]{1,0:T(8,128)(2,1)S(1)}, bf16[768,128]{1,0:T(8,128)(2,1)S(1)}, u32[]{:S(2)}, u32[]{:S(2)}) collective-permute-start(bf16[768,128]{1,0:T(8,128)(2,1)S(1)} %constant_dynamic-update-slice_fusion.27.a0), channel_id=1, source_target_pairs={{0,4},{4,0},{8,12},{12,8},{16,20},{20,16},{24,28},{28,24},{32,36},... | collective-permute-start | bytes 589832 | tf_op jit(solution)/shard_map/ppermute | solution.py:534
  91.1 2.4 %collective-permute-start.21 = (bf16[128,768]{1,0:T(8,128)(2,1)S(1)}, bf16[128,768]{1,0:T(8,128)(2,1)S(1)}, u32[]{:S(2)}, u32[]{:S(2)}) collective-permute-start(bf16[128,768]{1,0:T(8,128)(2,1)S(1)} %shard_map.101.t0), channel_id=1, source_target_pairs={{0,3},{1,2},{2,1},{3,0},{4,7},{5,6},{6,5},{7,4},{8,11},{9,10},{10,... | collective-permute-start | bytes 589832 | tf_op jit(solution)/shard_map/ppermute | solution.py:537
  94.5 5.5 %shard_map.100 = (bf16[512,384]{1,0:T(8,128)(2,1)S(1)}, bf16[384,768]{1,0:T(8,128)(2,1)S(1)}, bf16[384,768]{1,0:T(8,128)(2,1)S(1)}) custom-call(s32[2]{0:T(128)S(1)} %pad_add_fusion.idx.refs_0_, s32[4]{0:T(128)S(1)} %copy-done.5, bf16[256,768]{1,0:T(8,128)(2,1)S(1)} %constant_dynamic-update-slice_fusion.n0, bf16[256,768]{1,0:T(8,128)(2,1)S(1)} %collective-permute-done.1.n1, ...), custom_call_target="tpu_custom_call" | custom-call | flops 5000000000 | bytes 25000000 | tf_op jit(solution)/shard_map/pallas_call | solution.py:516
  100.0 3.2 %collective-permute-done.21.t3 = bf16[128,768]{1,0:T(8,128)(2,1)S(1)} collective-permute-done((bf16[128,768]{1,0:T(8,128)(2,1)S(1)}, bf16[128,768]{1,0:T(8,128)(2,1)S(1)}, u32[]{:S(2)}, u32[]{:S(2)}) %collective-permute-start.21) | collective-permute-done | bytes 196640 | tf_op jit(solution)/shard_map/ppermute | solution.py:537
  104.6 1.6 %shard_map.102 = bf16[512,768]{1,0:T(8,128)(2,1)} custom-call(bf16[512,192]{1,0:T(8,128)(2,1)S(1)} %get-tuple-element.99.gq, bf16[512,384]{1,0:T(8,128)(2,1)S(1)} %get-tuple-element.100.gkv, bf16[576,768]{1,0:T(8,128)(2,1)S(1)} %bitcast.5), custom_call_target="tpu_custom_call" | custom-call | flops 1000000000 | bytes 5000000 | tf_op jit(solution)/shard_map/pallas_call | solution.py:516
  106.5 1.2 collective-permute-start.25
  107.8 2.0 %collective-permute-start.24 = (bf16[96,768]{1,0:T(8,128)(2,1)S(1)}, bf16[96,768]{1,0:T(8,128)(2,1)S(1)}, u32[]{:S(2)}, u32[]{:S(2)}) collective-permute-start(bf16[96,768]{1,0:T(8,128)(2,1)S(1)} %get-tuple-element.122), channel_id=1, source_target_pairs={{0,16},{4,20},{8,24},{12,28},{16,0},{20,4},{24,8},{28,12},{32,48},... | collective-permute-start | bytes 442376 | tf_op jit(solution)/shard_map/ppermute | solution.py:534
  109.8 1.8 %collective-permute-done.23 = bf16[96,768]{1,0:T(8,128)(2,1)S(1)} collective-permute-done((bf16[96,768]{1,0:T(8,128)(2,1)S(1)}, bf16[96,768]{1,0:T(8,128)(2,1)S(1)}, u32[]{:S(2)}, u32[]{:S(2)}) %collective-permute-start.23) | collective-permute-done | bytes 147488 | tf_op jit(solution)/shard_map/ppermute | solution.py:534
  111.6 1.7 %collective-permute-done.25 = bf16[96,768]{1,0:T(8,128)(2,1)S(1)} collective-permute-done((bf16[96,768]{1,0:T(8,128)(2,1)S(1)}, bf16[96,768]{1,0:T(8,128)(2,1)S(1)}, u32[]{:S(2)}, u32[]{:S(2)}) %collective-permute-start.25) | collective-permute-done | bytes 147488 | tf_op jit(solution)/shard_map/ppermute | solution.py:534
  113.3 2.3 %collective-permute-done.24 = bf16[96,768]{1,0:T(8,128)(2,1)S(1)} collective-permute-done((bf16[96,768]{1,0:T(8,128)(2,1)S(1)}, bf16[96,768]{1,0:T(8,128)(2,1)S(1)}, u32[]{:S(2)}, u32[]{:S(2)}) %collective-permute-start.24) | collective-permute-done | bytes 147488 | tf_op jit(solution)/shard_map/ppermute | solution.py:534
  116.5 1.5 shard_map.103
  118.0 2.2 %collective-permute-done.26 = bf16[96,768]{1,0:T(8,128)(2,1)S(1)} collective-permute-done((bf16[96,768]{1,0:T(8,128)(2,1)S(1)}, bf16[96,768]{1,0:T(8,128)(2,1)S(1)}, u32[]{:S(2)}, u32[]{:S(2)}) %collective-permute-start.26) | collective-permute-done | bytes 147488 | tf_op jit(solution)/shard_map/ppermute | solution.py:534
  121.1 7.9 %collective-permute-done.27 = bf16[96,768]{1,0:T(8,128)(2,1)S(1)} collective-permute-done((bf16[96,768]{1,0:T(8,128)(2,1)S(1)}, bf16[96,768]{1,0:T(8,128)(2,1)S(1)}, u32[]{:S(2)}, u32[]{:S(2)}) %collective-permute-start.27) | collective-permute-done | bytes 147488 | tf_op jit(solution)/shard_map/ppermute | solution.py:534
  129.1 2.2 %collective-permute-start.28 = (bf16[96,768]{1,0:T(8,128)(2,1)S(1)}, bf16[96,768]{1,0:T(8,128)(2,1)S(1)}, u32[]{:S(2)}, u32[]{:S(2)}) collective-permute-start(bf16[96,768]{1,0:T(8,128)(2,1)S(1)} %add_convert_fusion.2), channel_id=1, source_target_pairs={{0,128},{4,132},{8,136},{12,140},{16,144},{20,148},{24,152},{28,15... | collective-permute-start | bytes 442376 | tf_op jit(solution)/shard_map/ppermute | solution.py:534
  134.5 1.9 %collective-permute-start.32 = (bf16[128,768]{1,0:T(8,128)(2,1)S(1)}, bf16[128,768]{1,0:T(8,128)(2,1)S(1)}, u32[]{:S(2)}, u32[]{:S(2)}) collective-permute-start(bf16[128,768]{1,0:T(8,128)(2,1)S(1)} %shard_map.104.t0), channel_id=1, source_target_pairs={{0,1},{1,0},{2,3},{3,2},{4,5},{5,4},{6,7},{7,6},{8,9},{9,8},{10,11... | collective-permute-start | bytes 589832 | tf_op jit(solution)/shard_map/ppermute | solution.py:537
  136.5 5.0 %collective-permute-done.28 = bf16[96,768]{1,0:T(8,128)(2,1)S(1)} collective-permute-done((bf16[96,768]{1,0:T(8,128)(2,1)S(1)}, bf16[96,768]{1,0:T(8,128)(2,1)S(1)}, u32[]{:S(2)}, u32[]{:S(2)}) %collective-permute-start.28) | collective-permute-done | bytes 147488 | tf_op jit(solution)/shard_map/ppermute | solution.py:534
  142.4 2.1 %collective-permute-done.34.t3 = bf16[128,768]{1,0:T(8,128)(2,1)S(1)} collective-permute-done((bf16[128,768]{1,0:T(8,128)(2,1)S(1)}, bf16[128,768]{1,0:T(8,128)(2,1)S(1)}, u32[]{:S(2)}, u32[]{:S(2)}) %collective-permute-start.34) | collective-permute-done | bytes 196640 | tf_op jit(solution)/shard_map/ppermute | solution.py:537
  144.5 1.2 collective-permute-start.29
  145.7 3.3 %collective-permute-done.31 = bf16[96,768]{1,0:T(8,128)(2,1)S(1)} collective-permute-done((bf16[96,768]{1,0:T(8,128)(2,1)S(1)}, bf16[96,768]{1,0:T(8,128)(2,1)S(1)}, u32[]{:S(2)}, u32[]{:S(2)}) %collective-permute-start.31) | collective-permute-done | bytes 147488 | tf_op jit(solution)/shard_map/ppermute | solution.py:534
  149.0 1.6 collective-permute-done.29
  150.6 2.3 %collective-permute-start.35 = (bf16[384,768]{1,0:T(8,128)(2,1)S(1)}, bf16[384,768]{1,0:T(8,128)(2,1)S(1)}, u32[]{:S(2)}, u32[]{:S(2)}) collective-permute-start(bf16[384,768]{1,0:T(8,128)(2,1)S(1)} %pad_maximum_fusion.refs_1_), channel_id=1, source_target_pairs={{0,4},{4,0},{8,12},{12,8},{16,20},{20,16},{24,28},{28,24},{32,36},... | collective-permute-start | bytes 1769480 | tf_op jit(solution)/shard_map/ppermute | solution.py:534
  152.9 1.5 shard_map.105
  154.6 2.1 %shard_map.106 = (f32[576,768]{1,0:T(8,128)}, f32[192,768]{1,0:T(8,128)}) custom-call(s32[2]{0:T(128)S(1)} %pad_add_fusion.idx.refs_0_, bf16[384,768]{1,0:T(8,128)(2,1)S(1)} %pad_maximum_fusion.refs_1_, bf16[384,768]{1,0:T(8,128)(2,1)S(1)} %collective-permute-done.35.refs_2_), custom_call_target="tpu_custom_call" | custom-call | flops 1000000000 | bytes 5000000 | tf_op jit(solution)/shard_map/pallas_call | solution.py:516
  (106 shorter events, 15.6 us)
Async XLA Ops:
  7.2 121.9 %reduce-scatter.2.cloned.1.call-start = ((), (), s32[]{:S(2)}) async-start(), calls=%async_computation.1 | async-start | bytes 983040 | tf_op jit(solution)/shard_map/reduce_scatter | solution.py:631
  7.9 1.1 copy-start.1
  9.1 1.3 copy-start
  9.1 1.4 copy-start.2
  9.1 1.5 copy-start.3
  10.5 12.7 %copy-start.5 = (s32[4]{0:T(128)S(1)}, s32[4]{0:T(128)}, u32[]{:S(2)}) copy-start(s32[4]{0:T(128)} %lens.11) | copy-start | bytes 52
  12.9 9.0 %collective-permute-start = (bf16[128,768]{1,0:T(8,128)(2,1)S(1)}, bf16[128,768]{1,0:T(8,128)(2,1)S(1)}, u32[]{:S(2)}, u32[]{:S(2)}) collective-permute-start(bf16[128,768]{1,0:T(8,128)(2,1)S(1)} %get-tuple-element.62), channel_id=1, source_target_pairs={{0,8},{4,12},{8,0},{12,4},{16,24},{20,28},{24,16},{28,20},{32,40},... | collective-permute-start | bytes 589832 | tf_op jit(solution)/shard_map/ppermute | solution.py:534
  14.9 11.2 %collective-permute-start.2 = (bf16[8,768]{1,0:T(8,128)(2,1)S(1)}, bf16[8,768]{1,0:T(8,128)(2,1)S(1)}, u32[]{:S(2)}, u32[]{:S(2)}) collective-permute-start(bf16[8,768]{1,0:T(8,128)(2,1)S(1)} %get-tuple-element.64), channel_id=1, source_target_pairs={{0,128},{4,132},{8,136},{12,140},{16,144},{20,148},{24,152},{28,15... | collective-permute-start | bytes 36872 | tf_op jit(solution)/shard_map/ppermute | solution.py:534
  21.9 8.8 %collective-permute-start.1 = (bf16[256,768]{1,0:T(8,128)(2,1)S(1)}, bf16[256,768]{1,0:T(8,128)(2,1)S(1)}, u32[]{:S(2)}, u32[]{:S(2)}) collective-permute-start(bf16[256,768]{1,0:T(8,128)(2,1)S(1)} %constant_dynamic-update-slice_fusion.n0), channel_id=1, source_target_pairs={{0,4},{4,0},{8,12},{12,8},{16,20},{20,16},{24,28},{28,24},{32,36},... | collective-permute-start | bytes 1179656 | tf_op jit(solution)/shard_map/ppermute | solution.py:534
  26.1 3.7 %collective-permute-start.3 = (bf16[16,768]{1,0:T(8,128)(2,1)S(1)}, bf16[16,768]{1,0:T(8,128)(2,1)S(1)}, u32[]{:S(2)}, u32[]{:S(2)}) collective-permute-start(bf16[16,768]{1,0:T(8,128)(2,1)S(1)} %pad_maximum_fusion.2), channel_id=1, source_target_pairs={{0,64},{4,68},{8,72},{12,76},{16,80},{20,84},{24,88},{28,92},{32,9... | collective-permute-start | bytes 73736 | tf_op jit(solution)/shard_map/ppermute | solution.py:534
  29.8 3.6 %collective-permute-start.4 = (bf16[64,768]{1,0:T(8,128)(2,1)S(1)}, bf16[64,768]{1,0:T(8,128)(2,1)S(1)}, u32[]{:S(2)}, u32[]{:S(2)}) collective-permute-start(bf16[64,768]{1,0:T(8,128)(2,1)S(1)} %pad_maximum_fusion.1), channel_id=1, source_target_pairs={{0,32},{4,36},{8,40},{12,44},{16,48},{20,52},{24,56},{28,60},{32,0... | collective-permute-start | bytes 294920 | tf_op jit(solution)/shard_map/ppermute | solution.py:534
  33.4 4.6 %collective-permute-start.5 = (bf16[128,768]{1,0:T(8,128)(2,1)S(1)}, bf16[128,768]{1,0:T(8,128)(2,1)S(1)}, u32[]{:S(2)}, u32[]{:S(2)}) collective-permute-start(bf16[128,768]{1,0:T(8,128)(2,1)S(1)} %get-tuple-element.123), channel_id=1, source_target_pairs={{0,8},{4,12},{8,0},{12,4},{16,24},{20,28},{24,16},{28,20},{32,40},... | collective-permute-start | bytes 589832 | tf_op jit(solution)/shard_map/ppermute | solution.py:534
  34.4 9.4 %collective-permute-start.7 = (bf16[128,768]{1,0:T(8,128)(2,1)S(1)}, bf16[128,768]{1,0:T(8,128)(2,1)S(1)}, u32[]{:S(2)}, u32[]{:S(2)}) collective-permute-start(bf16[128,768]{1,0:T(8,128)(2,1)S(1)} %get-tuple-element.123), channel_id=1, source_target_pairs={{0,24},{4,28},{8,16},{12,20},{16,8},{20,12},{24,0},{28,4},{32,56},... | collective-permute-start | bytes 589832 | tf_op jit(solution)/shard_map/ppermute | solution.py:534
  36.2 7.6 %collective-permute-start.6 = (bf16[128,768]{1,0:T(8,128)(2,1)S(1)}, bf16[128,768]{1,0:T(8,128)(2,1)S(1)}, u32[]{:S(2)}, u32[]{:S(2)}) collective-permute-start(bf16[128,768]{1,0:T(8,128)(2,1)S(1)} %get-tuple-element.123), channel_id=1, source_target_pairs={{0,16},{4,20},{8,24},{12,28},{16,0},{20,4},{24,8},{28,12},{32,48},... | collective-permute-start | bytes 589832 | tf_op jit(solution)/shard_map/ppermute | solution.py:534
  43.9 5.3 %collective-permute-start.8 = (bf16[512,768]{1,0:T(8,128)(2,1)S(1)}, bf16[512,768]{1,0:T(8,128)(2,1)S(1)}, u32[]{:S(2)}, u32[]{:S(2)}) collective-permute-start(bf16[512,768]{1,0:T(8,128)(2,1)S(1)} %slice_dynamic-update-slice_fusion.g0), channel_id=1, source_target_pairs={{0,4},{4,0},{8,12},{12,8},{16,20},{20,16},{24,28},{28,24},{32,36},... | collective-permute-start | bytes 2359304 | tf_op jit(solution)/shard_map/ppermute | solution.py:534
  52.2 14.2 %collective-permute-start.9 = (bf16[8,128]{1,0:T(8,128)(2,1)S(1)}, bf16[8,128]{1,0:T(8,128)(2,1)S(1)}, u32[]{:S(2)}, u32[]{:S(2)}) collective-permute-start(bf16[8,128]{1,0:T(8,128)(2,1)S(1)} %get-tuple-element.72), channel_id=1, source_target_pairs={{0,128},{4,132},{8,136},{12,140},{16,144},{20,148},{24,152},{28,15... | collective-permute-start | bytes 6152 | tf_op jit(solution)/shard_map/ppermute | solution.py:534
  57.6 15.4 %collective-permute-start.11 = (bf16[128,768]{1,0:T(8,128)(2,1)S(1)}, bf16[128,768]{1,0:T(8,128)(2,1)S(1)}, u32[]{:S(2)}, u32[]{:S(2)}) collective-permute-start(bf16[128,768]{1,0:T(8,128)(2,1)S(1)} %get-tuple-element.83), channel_id=1, source_target_pairs={{0,1},{1,0},{2,3},{3,2},{4,5},{5,4},{6,7},{7,6},{8,9},{9,8},{10,11... | collective-permute-start | bytes 589832 | tf_op jit(solution)/shard_map/ppermute | solution.py:537
  58.9 14.1 %collective-permute-start.12 = (bf16[128,768]{1,0:T(8,128)(2,1)S(1)}, bf16[128,768]{1,0:T(8,128)(2,1)S(1)}, u32[]{:S(2)}, u32[]{:S(2)}) collective-permute-start(bf16[128,768]{1,0:T(8,128)(2,1)S(1)} %get-tuple-element.84), channel_id=1, source_target_pairs={{0,3},{1,2},{2,1},{3,0},{4,7},{5,6},{6,5},{7,4},{8,11},{9,10},{10,... | collective-permute-start | bytes 589832 | tf_op jit(solution)/shard_map/ppermute | solution.py:537
  60.8 12.2 %collective-permute-start.13 = (bf16[128,768]{1,0:T(8,128)(2,1)S(1)}, bf16[128,768]{1,0:T(8,128)(2,1)S(1)}, u32[]{:S(2)}, u32[]{:S(2)}) collective-permute-start(bf16[128,768]{1,0:T(8,128)(2,1)S(1)} %get-tuple-element.85), channel_id=1, source_target_pairs={{0,2},{1,3},{2,0},{3,1},{4,6},{5,7},{6,4},{7,5},{8,10},{9,11},{10,... | collective-permute-start | bytes 589832 | tf_op jit(solution)/shard_map/ppermute | solution.py:537
  66.4 6.6 %collective-permute-start.10 = (bf16[16,128]{1,0:T(8,128)(2,1)S(1)}, bf16[16,128]{1,0:T(8,128)(2,1)S(1)}, u32[]{:S(2)}, u32[]{:S(2)}) collective-permute-start(bf16[16,128]{1,0:T(8,128)(2,1)S(1)} %pad_maximum_fusion.4), channel_id=1, source_target_pairs={{0,64},{4,68},{8,72},{12,76},{16,80},{20,84},{24,88},{28,92},{32,9... | collective-permute-start | bytes 12296 | tf_op jit(solution)/shard_map/ppermute | solution.py:534
  73.0 2.7 %collective-permute-start.14 = (bf16[64,128]{1,0:T(8,128)(2,1)S(1)}, bf16[64,128]{1,0:T(8,128)(2,1)S(1)}, u32[]{:S(2)}, u32[]{:S(2)}) collective-permute-start(bf16[64,128]{1,0:T(8,128)(2,1)S(1)} %pad_maximum_fusion.3), channel_id=1, source_target_pairs={{0,32},{4,36},{8,40},{12,44},{16,48},{20,52},{24,56},{28,60},{32,0... | collective-permute-start | bytes 49160 | tf_op jit(solution)/shard_map/ppermute | solution.py:534
  75.8 3.2 %collective-permute-start.15 = (bf16[256,128]{1,0:T(8,128)(2,1)S(1)}, bf16[256,128]{1,0:T(8,128)(2,1)S(1)}, u32[]{:S(2)}, u32[]{:S(2)}) collective-permute-start(bf16[256,128]{1,0:T(8,128)(2,1)S(1)} %get-tuple-element.127), channel_id=1, source_target_pairs={{0,8},{4,12},{8,0},{12,4},{16,24},{20,28},{24,16},{28,20},{32,40},... | collective-permute-start | bytes 196616 | tf_op jit(solution)/shard_map/ppermute | solution.py:534
  79.0 5.9 %collective-permute-start.17 = (bf16[128,128]{1,0:T(8,128)(2,1)S(1)}, bf16[128,128]{1,0:T(8,128)(2,1)S(1)}, u32[]{:S(2)}, u32[]{:S(2)}) collective-permute-start(bf16[128,128]{1,0:T(8,128)(2,1)S(1)} %get-tuple-element.129), channel_id=1, source_target_pairs={{0,24},{4,28},{8,16},{12,20},{16,8},{20,12},{24,0},{28,4},{32,56},... | collective-permute-start | bytes 98312 | tf_op jit(solution)/shard_map/ppermute | solution.py:534
  80.6 4.3 %collective-permute-start.16 = (bf16[128,128]{1,0:T(8,128)(2,1)S(1)}, bf16[128,128]{1,0:T(8,128)(2,1)S(1)}, u32[]{:S(2)}, u32[]{:S(2)}) collective-permute-start(bf16[128,128]{1,0:T(8,128)(2,1)S(1)} %get-tuple-element.129), channel_id=1, source_target_pairs={{0,16},{4,20},{8,24},{12,28},{16,0},{20,4},{24,8},{28,12},{32,48},... | collective-permute-start | bytes 98312 | tf_op jit(solution)/shard_map/ppermute | solution.py:534
  85.0 9.5 %collective-permute-start.18 = (bf16[768,128]{1,0:T(8,128)(2,1)S(1)}, bf16[768,128]{1,0:T(8,128)(2,1)S(1)}, u32[]{:S(2)}, u32[]{:S(2)}) collective-permute-start(bf16[768,128]{1,0:T(8,128)(2,1)S(1)} %constant_dynamic-update-slice_fusion.27.a0), channel_id=1, source_target_pairs={{0,4},{4,0},{8,12},{12,8},{16,20},{20,16},{24,28},{28,24},{32,36},... | collective-permute-start | bytes 589832 | tf_op jit(solution)/shard_map/ppermute | solution.py:534
  91.1 12.0 %collective-permute-start.21 = (bf16[128,768]{1,0:T(8,128)(2,1)S(1)}, bf16[128,768]{1,0:T(8,128)(2,1)S(1)}, u32[]{:S(2)}, u32[]{:S(2)}) collective-permute-start(bf16[128,768]{1,0:T(8,128)(2,1)S(1)} %shard_map.101.t0), channel_id=1, source_target_pairs={{0,3},{1,2},{2,1},{3,0},{4,7},{5,6},{6,5},{7,4},{8,11},{9,10},{10,... | collective-permute-start | bytes 589832 | tf_op jit(solution)/shard_map/ppermute | solution.py:537
  93.6 9.6 %collective-permute-start.20 = (bf16[128,768]{1,0:T(8,128)(2,1)S(1)}, bf16[128,768]{1,0:T(8,128)(2,1)S(1)}, u32[]{:S(2)}, u32[]{:S(2)}) collective-permute-start(bf16[128,768]{1,0:T(8,128)(2,1)S(1)} %shard_map.101.t0), channel_id=1, source_target_pairs={{0,2},{1,3},{2,0},{3,1},{4,6},{5,7},{6,4},{7,5},{8,10},{9,11},{10,... | collective-permute-start | bytes 589832 | tf_op jit(solution)/shard_map/ppermute | solution.py:537
  93.9 9.6 %collective-permute-start.19 = (bf16[128,768]{1,0:T(8,128)(2,1)S(1)}, bf16[128,768]{1,0:T(8,128)(2,1)S(1)}, u32[]{:S(2)}, u32[]{:S(2)}) collective-permute-start(bf16[128,768]{1,0:T(8,128)(2,1)S(1)} %shard_map.101.t0), channel_id=1, source_target_pairs={{0,1},{1,0},{2,3},{3,2},{4,5},{5,4},{6,7},{7,6},{8,9},{9,8},{10,11... | collective-permute-start | bytes 589832 | tf_op jit(solution)/shard_map/ppermute | solution.py:537
  103.5 2.8 %collective-permute-start.22 = (bf16[384,768]{1,0:T(8,128)(2,1)S(1)}, bf16[384,768]{1,0:T(8,128)(2,1)S(1)}, u32[]{:S(2)}, u32[]{:S(2)}) collective-permute-start(bf16[384,768]{1,0:T(8,128)(2,1)S(1)} %get-tuple-element.98), channel_id=1, source_target_pairs={{0,4},{4,0},{8,12},{12,8},{16,20},{20,16},{24,28},{28,24},{32,36},... | collective-permute-start | bytes 1769480 | tf_op jit(solution)/shard_map/ppermute | solution.py:534
  106.4 5.2 %collective-permute-start.23 = (bf16[96,768]{1,0:T(8,128)(2,1)S(1)}, bf16[96,768]{1,0:T(8,128)(2,1)S(1)}, u32[]{:S(2)}, u32[]{:S(2)}) collective-permute-start(bf16[96,768]{1,0:T(8,128)(2,1)S(1)} %get-tuple-element.120), channel_id=1, source_target_pairs={{0,8},{4,12},{8,0},{12,4},{16,24},{20,28},{24,16},{28,20},{32,40},... | collective-permute-start | bytes 442376 | tf_op jit(solution)/shard_map/ppermute | solution.py:534
  106.5 6.8 %collective-permute-start.25 = (bf16[96,768]{1,0:T(8,128)(2,1)S(1)}, bf16[96,768]{1,0:T(8,128)(2,1)S(1)}, u32[]{:S(2)}, u32[]{:S(2)}) collective-permute-start(bf16[96,768]{1,0:T(8,128)(2,1)S(1)} %get-tuple-element.121), channel_id=1, source_target_pairs={{0,24},{4,28},{8,16},{12,20},{16,8},{20,12},{24,0},{28,4},{32,56},... | collective-permute-start | bytes 442376 | tf_op jit(solution)/shard_map/ppermute | solution.py:534
  107.8 7.9 %collective-permute-start.24 = (bf16[96,768]{1,0:T(8,128)(2,1)S(1)}, bf16[96,768]{1,0:T(8,128)(2,1)S(1)}, u32[]{:S(2)}, u32[]{:S(2)}) collective-permute-start(bf16[96,768]{1,0:T(8,128)(2,1)S(1)} %get-tuple-element.122), channel_id=1, source_target_pairs={{0,16},{4,20},{8,24},{12,28},{16,0},{20,4},{24,8},{28,12},{32,48},... | collective-permute-start | bytes 442376 | tf_op jit(solution)/shard_map/ppermute | solution.py:534
  115.8 4.5 %collective-permute-start.26 = (bf16[96,768]{1,0:T(8,128)(2,1)S(1)}, bf16[96,768]{1,0:T(8,128)(2,1)S(1)}, u32[]{:S(2)}, u32[]{:S(2)}) collective-permute-start(bf16[96,768]{1,0:T(8,128)(2,1)S(1)} %add_convert_fusion.4), channel_id=1, source_target_pairs={{0,32},{4,36},{8,40},{12,44},{16,48},{20,52},{24,56},{28,60},{32,0... | collective-permute-start | bytes 442376 | tf_op jit(solution)/shard_map/ppermute | solution.py:534
  120.3 8.7 %collective-permute-start.27 = (bf16[96,768]{1,0:T(8,128)(2,1)S(1)}, bf16[96,768]{1,0:T(8,128)(2,1)S(1)}, u32[]{:S(2)}, u32[]{:S(2)}) collective-permute-start(bf16[96,768]{1,0:T(8,128)(2,1)S(1)} %add_convert_fusion.3), channel_id=1, source_target_pairs={{0,64},{4,68},{8,72},{12,76},{16,80},{20,84},{24,88},{28,92},{32,9... | collective-permute-start | bytes 442376 | tf_op jit(solution)/shard_map/ppermute | solution.py:534
  129.1 12.4 %collective-permute-start.28 = (bf16[96,768]{1,0:T(8,128)(2,1)S(1)}, bf16[96,768]{1,0:T(8,128)(2,1)S(1)}, u32[]{:S(2)}, u32[]{:S(2)}) collective-permute-start(bf16[96,768]{1,0:T(8,128)(2,1)S(1)} %add_convert_fusion.2), channel_id=1, source_target_pairs={{0,128},{4,132},{8,136},{12,140},{16,144},{20,148},{24,152},{28,15... | collective-permute-start | bytes 442376 | tf_op jit(solution)/shard_map/ppermute | solution.py:534
  131.3 0.9 copy-start.4
  133.1 11.4 %collective-permute-start.34 = (bf16[128,768]{1,0:T(8,128)(2,1)S(1)}, bf16[128,768]{1,0:T(8,128)(2,1)S(1)}, u32[]{:S(2)}, u32[]{:S(2)}) collective-permute-start(bf16[128,768]{1,0:T(8,128)(2,1)S(1)} %shard_map.104.t0), channel_id=1, source_target_pairs={{0,3},{1,2},{2,1},{3,0},{4,7},{5,6},{6,5},{7,4},{8,11},{9,10},{10,... | collective-permute-start | bytes 589832 | tf_op jit(solution)/shard_map/ppermute | solution.py:537
  133.8 12.0 %collective-permute-start.33 = (bf16[128,768]{1,0:T(8,128)(2,1)S(1)}, bf16[128,768]{1,0:T(8,128)(2,1)S(1)}, u32[]{:S(2)}, u32[]{:S(2)}) collective-permute-start(bf16[128,768]{1,0:T(8,128)(2,1)S(1)} %shard_map.104.t0), channel_id=1, source_target_pairs={{0,2},{1,3},{2,0},{3,1},{4,6},{5,7},{6,4},{7,5},{8,10},{9,11},{10,... | collective-permute-start | bytes 589832 | tf_op jit(solution)/shard_map/ppermute | solution.py:537
  134.5 11.2 %collective-permute-start.32 = (bf16[128,768]{1,0:T(8,128)(2,1)S(1)}, bf16[128,768]{1,0:T(8,128)(2,1)S(1)}, u32[]{:S(2)}, u32[]{:S(2)}) collective-permute-start(bf16[128,768]{1,0:T(8,128)(2,1)S(1)} %shard_map.104.t0), channel_id=1, source_target_pairs={{0,1},{1,0},{2,3},{3,2},{4,5},{5,4},{6,7},{7,6},{8,9},{9,8},{10,11... | collective-permute-start | bytes 589832 | tf_op jit(solution)/shard_map/ppermute | solution.py:537
  141.5 7.5 %collective-permute-start.31 = (bf16[96,768]{1,0:T(8,128)(2,1)S(1)}, bf16[96,768]{1,0:T(8,128)(2,1)S(1)}, u32[]{:S(2)}, u32[]{:S(2)}) collective-permute-start(bf16[96,768]{1,0:T(8,128)(2,1)S(1)} %add_convert_fusion.1), channel_id=1, source_target_pairs={{0,24},{4,28},{8,16},{12,20},{16,8},{20,12},{24,0},{28,4},{32,56},... | collective-permute-start | bytes 442376 | tf_op jit(solution)/shard_map/ppermute | solution.py:534
  142.4 6.6 %collective-permute-start.30 = (bf16[96,768]{1,0:T(8,128)(2,1)S(1)}, bf16[96,768]{1,0:T(8,128)(2,1)S(1)}, u32[]{:S(2)}, u32[]{:S(2)}) collective-permute-start(bf16[96,768]{1,0:T(8,128)(2,1)S(1)} %add_convert_fusion.1), channel_id=1, source_target_pairs={{0,16},{4,20},{8,24},{12,28},{16,0},{20,4},{24,8},{28,12},{32,48},... | collective-permute-start | bytes 442376 | tf_op jit(solution)/shard_map/ppermute | solution.py:534
  144.5 6.1 %collective-permute-start.29 = (bf16[96,768]{1,0:T(8,128)(2,1)S(1)}, bf16[96,768]{1,0:T(8,128)(2,1)S(1)}, u32[]{:S(2)}, u32[]{:S(2)}) collective-permute-start(bf16[96,768]{1,0:T(8,128)(2,1)S(1)} %add_convert_fusion.1), channel_id=1, source_target_pairs={{0,8},{4,12},{8,0},{12,4},{16,24},{20,28},{24,16},{28,20},{32,40},... | collective-permute-start | bytes 442376 | tf_op jit(solution)/shard_map/ppermute | solution.py:534
  150.6 3.9 %collective-permute-start.35 = (bf16[384,768]{1,0:T(8,128)(2,1)S(1)}, bf16[384,768]{1,0:T(8,128)(2,1)S(1)}, u32[]{:S(2)}, u32[]{:S(2)}) collective-permute-start(bf16[384,768]{1,0:T(8,128)(2,1)S(1)} %pad_maximum_fusion.refs_1_), channel_id=1, source_target_pairs={{0,4},{4,0},{8,12},{12,8},{16,20},{20,16},{24,28},{28,24},{32,36},... | collective-permute-start | bytes 1769480 | tf_op jit(solution)/shard_map/ppermute | solution.py:534
Sparse Core Ops, SparseCore 0:
  106.4 19.3 reduce-scatter.1
